TPU v7x, 128 devices: a whole 4x4x4 slice. The times are simulated.
128 devices in a mesh: pipe: 4 (over x_hi, core), seq: 32 (over x_lo, y, z).
Axes of the slice: x: 4 (x_hi: 2, x_lo: 2; x = x_hi * 2 + x_lo), y: 4, z: 4, core: 2. Of those that a mesh axis runs over, the one named last changes fastest.
Arguments:
- queries: bfloat16 [4, 4096, 4096], P('pipe', 'seq'), may hold values from -11 to 11
- shared_keys: bfloat16 [4096, 512], P('seq', 'pipe'), may hold values from -6 to 6
- shared_values: bfloat16 [4096, 512], P('seq', 'pipe'), may hold values from -6 to 6
- out_grad: bfloat16 [4, 4096, 4096], P('pipe', 'seq'), may hold values from -6 to 6
Outputs:
- query_grad: bfloat16 [4, 4096, 4096], P('pipe', 'seq')
- key_grad: bfloat16 [4096, 512], P('seq', 'pipe')
- value_grad: bfloat16 [4096, 512], P('seq', 'pipe')
All inputs are finite; a program needn't handle non-finite values.
Results may differ from a plain program's by a relative error of at most 0.006.
Values may be sent and summed in bfloat16 or wider, within the bound.
A program may use at most 128 MiB of HBM per device.

v0:
```python
import math

import jax
import jax.numpy as jnp
from jax import lax
from jax.sharding import PartitionSpec as P

DH = 128


def body(queries, shared_keys, shared_values, out_grad):
    query_rows = queries[0]
    cotangent = out_grad[0]
    tok_count = query_rows.shape[0]
    seq_index = lax.axis_index("seq")
    head_keys, head_values = (
        lax.all_gather(shared_keys, "pipe", axis=1, tiled=True),
        lax.all_gather(shared_values, "pipe", axis=1, tiled=True),
    )
    full_keys, full_values = (
        lax.all_gather(head_keys, "seq", axis=0, tiled=True),
        lax.all_gather(head_values, "seq", axis=0, tiled=True),
    )
    total_rows = full_keys.shape[0]
    kv_width = full_keys.shape[1]
    kv_heads = kv_width // DH
    group_size = query_rows.shape[1] // DH // kv_heads
    block_rows = min(512, total_rows)
    scale = 1.0 / math.sqrt(DH)
    query_heads = query_rows.reshape(tok_count, kv_heads, group_size, DH)
    grad_heads = cotangent.reshape(tok_count, kv_heads, group_size, DH)
    query_pos = seq_index * tok_count + jnp.arange(tok_count, dtype=jnp.int32)
    block_count = ((seq_index + 1) * tok_count + block_rows - 1) // block_rows

    def block_terms(start):
        key_block = lax.dynamic_slice_in_dim(full_keys, start, block_rows, 0).reshape(
            block_rows, kv_heads, DH
        )
        value_block = lax.dynamic_slice_in_dim(full_values, start, block_rows, 0).reshape(
            block_rows, kv_heads, DH
        )
        scores = (
            jnp.einsum("tkgd,jkd->kgtj", query_heads, key_block, preferred_element_type=jnp.float32)
            * scale
        )
        key_pos = start + jnp.arange(block_rows, dtype=jnp.int32)
        visible = query_pos[:, None] >= key_pos[None, :]
        scores = jnp.where(visible, scores, jnp.float32(-1e30))
        prob_grad = jnp.einsum(
            "tkgd,jkd->kgtj", grad_heads, value_block, preferred_element_type=jnp.float32
        )
        return (key_block, scores, visible, prob_grad)

    def stats_step(index, carry):
        run_max, run_sum, run_dot = carry
        key_block, scores, visible, prob_grad = block_terms(index * block_rows)
        new_max = jnp.maximum(run_max, jnp.max(scores, axis=-1))
        rescale = jnp.exp(run_max - new_max)
        weights = jnp.where(visible, jnp.exp(scores - new_max[..., None]), jnp.float32(0.0))
        new_sum = run_sum * rescale + jnp.sum(weights, axis=-1)
        new_dot = run_dot * rescale + jnp.sum(weights * prob_grad, axis=-1)
        return (new_max, new_sum, new_dot)

    stat_shape = (kv_heads, group_size, tok_count)
    stats_init = (
        jnp.full(stat_shape, -1e30, jnp.float32),
        jnp.zeros(stat_shape, jnp.float32),
        jnp.zeros(stat_shape, jnp.float32),
    )
    run_max, run_sum, run_dot = lax.fori_loop(0, block_count, stats_step, stats_init)
    row_dot = run_dot / run_sum

    def grad_step(index, carry):
        query_acc, key_part, value_part = carry
        start = index * block_rows
        key_block, scores, visible, prob_grad = block_terms(start)
        probs = jnp.where(
            visible, jnp.exp(scores - run_max[..., None]) / run_sum[..., None], jnp.float32(0.0)
        )
        score_grad = probs * (prob_grad - row_dot[..., None])
        probs_low = probs.astype(jnp.bfloat16)
        score_low = score_grad.astype(jnp.bfloat16)
        value_block_grad = jnp.einsum(
            "kgtj,tkgd->jkd", probs_low, grad_heads, preferred_element_type=jnp.float32
        ).reshape(block_rows, kv_width)
        key_block_grad = (
            jnp.einsum(
                "kgtj,tkgd->jkd", score_low, query_heads, preferred_element_type=jnp.float32
            ).reshape(block_rows, kv_width)
            * scale
        )
        query_acc = query_acc + jnp.einsum(
            "kgtj,jkd->tkgd", score_low, key_block, preferred_element_type=jnp.float32
        )
        key_part = lax.dynamic_update_slice_in_dim(key_part, key_block_grad, start, 0)
        value_part = lax.dynamic_update_slice_in_dim(value_part, value_block_grad, start, 0)
        return (query_acc, key_part, value_part)

    grad_init = (
        jnp.zeros((tok_count, kv_heads, group_size, DH), jnp.float32),
        jnp.zeros((total_rows, kv_width), jnp.float32),
        jnp.zeros((total_rows, kv_width), jnp.float32),
    )
    query_acc, key_part, value_part = lax.fori_loop(0, block_count, grad_step, grad_init)
    query_grad = (query_acc * scale).astype(jnp.bfloat16).reshape(1, tok_count, query_rows.shape[1])
    key_rows, value_rows = (
        lax.psum_scatter(key_part, "seq", scatter_dimension=0, tiled=True),
        lax.psum_scatter(value_part, "seq", scatter_dimension=0, tiled=True),
    )
    key_sum, value_sum = (
        lax.psum_scatter(key_rows, "pipe", scatter_dimension=1, tiled=True),
        lax.psum_scatter(value_rows, "pipe", scatter_dimension=1, tiled=True),
    )
    return (query_grad, key_sum.astype(jnp.bfloat16), value_sum.astype(jnp.bfloat16))


def solution(mesh):
    return jax.shard_map(
        body,
        mesh=mesh,
        in_specs=(
            P("pipe", "seq", None),
            P("seq", "pipe"),
            P("seq", "pipe"),
            P("pipe", "seq", None),
        ),
        out_specs=(P("pipe", "seq", None), P("seq", "pipe"), P("seq", "pipe")),
        check_vma=False,
    )
```

profile of v0, /device:TPU:1, one launch (start us, length us, event | category | flops | bytes accessed | tf_op | source)
XLA Modules:
  0.0 972.4 jit_solution(16038559115098106074)
XLA Ops:
  7.2 0.0 all-gather.5.cloned.1.call-start
  7.2 0.9 copy.31
  8.1 8.6 all_gather.14
  16.7 0.0 all-gather.3.cloned.1.call-start
  16.8 0.9 copy.29
  17.7 7.4 all_gather.12
  25.1 0.0 reduce-scatter.9.cloned.1.call-start
  25.1 2.3 copy.30
  27.4 1.6 copy.33
  29.0 2.3 copy.32
  31.3 1.6 copy.34
  32.9 105.8 %all-gather.5.cloned.1.call-done = bf16[4096,512]{0,1:T(8,128)(2,1)} async-done(((bf16[128,512]{0,1:T(8,128)(2,1)}), bf16[4096,512]{0,1:T(8,128)(2,1)}) %all-gather.5.cloned.1.call-update) | async-done | bytes 4194320 | tf_op jit(solution)/shard_map/all_gather | solution.py:22
  138.7 139.7 %all-gather.3.cloned.1.call-done = bf16[4096,512]{0,1:T(8,128)(2,1)} async-done(((bf16[128,512]{0,1:T(8,128)(2,1)}), bf16[4096,512]{0,1:T(8,128)(2,1)}) %all-gather.3.cloned.1.call-update) | async-done | bytes 4194320 | tf_op jit(solution)/shard_map/all_gather | solution.py:21
  278.4 8.1 while.30
  278.4 0.1 broadcast_compare_fusion.4
  278.6 1.3 constant_dynamic-slice_fusion.7
  279.9 1.4 fusion.54
  281.3 3.0 fusion.55
  284.3 2.1 fusion.56
  286.5 1.6 broadcast_in_dim.36
  288.1 4.3 broadcast.38.clone2
  292.4 4.3 broadcast.38.clone
  296.7 22.6 %while.31 = (s32[]{:T(128)}, f32[128,4,8,128]{0,3,2,1:T(8,128)}, f32[4096,512]{1,0:T(8,128)}, f32[4096,512]{1,0:T(8,128)}, s32[]{:T(128)}, /*index=5*/bf16[4096,...) while((s32[]{:T(128)}, f32[128,4,8,128]{0,3,2,1:T(8,128)}, ...), condition=%wide.region_6.7_spmd.clone, body=%wide.region_5.6_spmd.clone.sunk | while | flops 2704081408 | bytes 94033200 | solution.py:104
  296.7 0.1 broadcast_compare_fusion.5
  296.8 1.1 constant_dynamic-slice_fusion.9
  297.9 1.1 constant_dynamic-slice_fusion.8
  299.0 3.8 fusion.67
  302.8 2.7 fusion.69
  305.5 4.6 fusion.68
  310.1 0.3 copy.65
  310.5 4.1 fusion.70
  314.6 0.3 copy-done.1
  314.9 1.3 bitcast_add_fusion.2
  316.2 1.3 copy-done.2
  317.5 0.3 copy.66
  317.8 1.5 constant_dynamic-update-slice_fusion.3
  319.3 0.0 reduce-scatter.5.cloned.1.call-start
  319.4 0.5 reduce-scatter.5.cloned.1.call-update
  319.9 0.0 reduce-scatter.11.cloned.1.call-start
  319.9 389.5 %reduce-scatter.9.cloned.1.call-done = f32[128,512]{1,0:T(8,128)} async-done(((f32[4096,512]{1,0:T(8,128)}), f32[128,512]{1,0:T(8,128)}) %reduce-scatter.9.cloned.1.call-update) | async-done | bytes 262160 | tf_op jit(solution)/shard_map/reduce_scatter | solution.py:108
  709.4 0.0 reduce-scatter.7.cloned.1.call-start
  709.5 177.1 %reduce-scatter.5.cloned.1.call-done = f32[128,512]{1,0:T(8,128)} async-done(((f32[4096,512]{1,0:T(8,128)}), f32[128,512]{1,0:T(8,128)}) %reduce-scatter.5.cloned.1.call-update) | async-done | bytes 262160 | tf_op jit(solution)/shard_map/reduce_scatter | solution.py:107
  886.6 0.3 multiply_convert_fusion
  886.9 1.3 copy.50
  888.2 46.9 %reduce-scatter.11.cloned.1.call-done = f32[128,128]{1,0:T(8,128)} async-done(((f32[128,512]{1,0:T(8,128)}), f32[128,128]{1,0:T(8,128)}) %reduce-scatter.11.cloned.1.call-update) | async-done | bytes 65552 | tf_op jit(solution)/shard_map/reduce_scatter | solution.py:112
  935.2 1.5 convert_element_type.17
  936.6 27.5 %reduce-scatter.7.cloned.1.call-done = f32[128,128]{1,0:T(8,128)} async-done(((f32[128,512]{1,0:T(8,128)}), f32[128,128]{1,0:T(8,128)}) %reduce-scatter.7.cloned.1.call-update) | async-done | bytes 65552 | tf_op jit(solution)/shard_map/reduce_scatter | solution.py:111
  964.1 1.5 convert_element_type.16
  (22 shorter events, 0.1 us)
Async XLA Ops:
  7.2 131.5 %all-gather.5.cloned.1.call-start = ((), (), s32[]{:S(2)}) async-start(), calls=%async_computation.5 | async-start | bytes 4325376 | tf_op jit(solution)/shard_map/all_gather | solution.py:22
  16.7 261.7 %all-gather.3.cloned.1.call-start = ((), (), s32[]{:S(2)}) async-start(), calls=%async_computation.4 | async-start | bytes 4325376 | tf_op jit(solution)/shard_map/all_gather | solution.py:21
  25.1 684.4 %reduce-scatter.9.cloned.1.call-start = ((), (), s32[]{:S(2)}) async-start(), calls=%async_computation.8 | async-start | bytes 8650752 | tf_op jit(solution)/shard_map/reduce_scatter | solution.py:108
  310.4 4.2 copy-start
  310.4 4.4 copy-start.1
  316.2 1.3 copy-start.2
  319.3 567.3 %copy-start.3 = (f32[128,4,8,128]{0,3,2,1:T(8,128)S(1)}, f32[128,4,8,128]{0,3,2,1:T(8,128)}, u32[]{:S(2)}) copy-start(f32[128,4,8,128]{0,3,2,1:T(8,128)} %get-tuple-element.131) | copy-start | bytes 6291460
  319.3 567.3 %reduce-scatter.5.cloned.1.call-start = ((), (), s32[]{:S(2)}) async-start(), calls=%async_computation.6 | async-start | bytes 8650752 | tf_op jit(solution)/shard_map/reduce_scatter | solution.py:107
  319.9 615.3 %reduce-scatter.11.cloned.1.call-start = ((), (), s32[]{:S(2)}) async-start(), calls=%async_computation.9 | async-start | bytes 327680 | tf_op jit(solution)/shard_map/reduce_scatter | solution.py:112
  709.4 254.7 %reduce-scatter.7.cloned.1.call-start = ((), (), s32[]{:S(2)}) async-start(), calls=%async_computation.7 | async-start | bytes 327680 | tf_op jit(solution)/shard_map/reduce_scatter | solution.py:111
Sparse Core Ops, SparseCore 0:
  16.9 121.7 all-gather.4
  140.2 138.0 all-gather.2
  319.4 389.9 reduce-scatter.8
  711.7 174.8 reduce-scatter.4
  889.0 46.1 reduce-scatter.10
  937.7 26.3 reduce-scatter.6
where the time goes:
time: 975 us; the launch traced here: 972 us
  waiting for transfers between devices  887 us (91%)
  local copies, waits for them, and re-layouts  28.2 us (3%)
  matrix products  20.9 us (2%)
  blocking collectives  16 us (2%)
  between operations  14.2 us (1%)
    reduce_scatter x1, waiting for transfers between devices, body(): lax.psum_scatter(value_part, 'seq', scatter_dimension=0, tiled=True)  389 us
    reduce_scatter x1, waiting for transfers between devices, body(): lax.psum_scatter(key_part, 'seq', scatter_dimension=0, tiled=True)  177 us
    all_gather x1, waiting for transfers between devices, body(): lax.all_gather(head_keys, 'seq', axis=0, tiled=True)  140 us
    all_gather x1, waiting for transfers between devices, body(): lax.all_gather(head_values, 'seq', axis=0, tiled=True)  106 us
    reduce_scatter x1, waiting for transfers between devices, body(): lax.psum_scatter(value_rows, 'pipe', scatter_dimension=1, tiled=True)  46.9 us
    reduce_scatter x1, waiting for transfers between devices, body(): lax.psum_scatter(key_rows, 'pipe', scatter_dimension=1, tiled=True)  27.5 us
  transfers between devices with their start and end apart: 6, of which 6 were waited for; matrix products, arithmetic and copies ran while one was open for 1% of the time, Pallas kernels for 0%

commit v1 on v0

v1 whole, which is shorter than its diff:
```python
import functools
import math

import jax
import jax.numpy as jnp
from jax import lax
from jax.experimental import pallas as pl
from jax.experimental.pallas import tpu as pltpu
from jax.sharding import PartitionSpec as P

DH = 128
TOK = 128
CH = 256
SCALE = 1.0 / math.sqrt(DH)
EXPO = math.log2(math.e) / math.sqrt(DH)
f32, bf16 = jnp.float32, jnp.bfloat16
NN = (((1,), (0,)), ((), ()))


def dot(a, b):
    return lax.dot_general(a, b, NN, preferred_element_type=f32)


def lanes(start, size):
    return pl.ds(pl.multiple_of(start, 128), size)


def kernel(
    q_in, k_in, v_in, g_in,
    dq_out, dk_out, dv_out,
    q_s, g_s, dq_s, kv, q_t, g_t, k_t, acc, dkv,
    m8, l8, d8, top, rdot,
    st1, rc1, st2, rc2, red, st3, rc3, st4, rc4, fin, rcx,
    ex_send, ex_recv, loc, a_send, a_recv, ag_send, ag_recv,
    rs_send, rs_recv, x_send, x_recv, dq_send, dq_recv,
):
    pipe = lax.axis_index("pipe")
    seq = lax.axis_index("seq")
    x_hi, core = pipe // 2, pipe % 2
    x_lo, y, z = seq // 16, (seq // 4) % 4, seq % 4
    head = 2 * x_lo + core

    def dev(x_hi_, core_, x_lo_, y_, z_):
        return {"pipe": x_hi_ * 2 + core_, "seq": x_lo_ * 16 + y_ * 4 + z_}

    def remote(src, dst, send, recv, to):
        return pltpu.make_async_remote_copy(
            src_ref=src, dst_ref=dst, send_sem=send, recv_sem=recv,
            device_id=to, device_id_type=pl.DeviceIdType.MESH,
        )

    mates = [
        dev(x_hi, 1 - core, x_lo, y, z),
        dev(x_hi, core, 1 - x_lo, 3 - y, 3 - z),
        dev(x_hi, 1 - core, 1 - x_lo, 3 - y, 3 - z),
    ]
    y_up, y_dn = dev(x_hi, core, x_lo, (y + 1) % 4, z), dev(x_hi, core, x_lo, (y + 3) % 4, z)
    z_up, z_dn = dev(x_hi, core, x_lo, y, (z + 1) % 4), dev(x_hi, core, x_lo, y, (z + 3) % 4)
    ring = ((y_up, y_dn), (z_up, z_dn))

    def x_to(t):
        return dev(t, core, x_hi, y, z)

    def x_from(s):
        return dev(x_lo, core, s, y, z)

    barrier = pltpu.get_barrier_semaphore()
    for peer in mates + [y_up, y_dn, z_up, z_dn]:
        pl.semaphore_signal(barrier, inc=1, device_id=peer, device_id_type=pl.DeviceIdType.MESH)
    for t in range(2):
        @pl.when(jnp.logical_not(jnp.logical_and(t == x_hi, x_lo == x_hi)))
        def _():
            pl.semaphore_signal(barrier, inc=1, device_id=x_to(t), device_id_type=pl.DeviceIdType.MESH)

        @pl.when(jnp.logical_not(jnp.logical_and(x_lo == x_hi, t == x_lo)))
        def _():
            pl.semaphore_signal(barrier, inc=1, device_id=x_from(t), device_id_type=pl.DeviceIdType.MESH)

    @pl.when(x_hi == x_lo)
    def _():
        pl.semaphore_wait(barrier, 9)

    @pl.when(x_hi != x_lo)
    def _():
        pl.semaphore_wait(barrier, 11)

    def a_copies(t):
        to_self = jnp.logical_and(t == x_hi, x_lo == x_hi)
        pairs = []
        for i, src in enumerate((k_in, v_in)):
            dst = kv.at[i, x_lo, y, z]
            pairs.append((
                pltpu.make_async_copy(src, dst, a_recv.at[i, x_lo]),
                remote(src, dst, a_send.at[i, t], a_recv.at[i, x_lo], x_to(t)),
            ))
        return to_self, pairs

    for t in range(2):
        to_self, pairs = a_copies(t)
        for local, away in pairs:
            @pl.when(to_self)
            def _(local=local):
                local.start()

            @pl.when(jnp.logical_not(to_self))
            def _(away=away):
                away.start()

    ex = []
    for n, (c_t, flip) in enumerate(((1 - core, 0), (core, 1), (1 - core, 1))):
        x_t = (1 - x_lo) if flip else x_lo
        cols = lanes((2 * x_t + c_t) * 1024, 1024)
        slot = 2 * flip + core
        for i, (src, dst) in enumerate(((q_in, q_s), (g_in, g_s))):
            ex.append(remote(src.at[:, cols], dst.at[slot], ex_send.at[i, n], ex_recv.at[i, n], mates[n]))
    for copy in ex:
        copy.start()
    own_cols = lanes(head * 1024, 1024)
    own = [
        pltpu.make_async_copy(q_in.at[:, own_cols], q_s.at[core], loc.at[0]),
        pltpu.make_async_copy(g_in.at[:, own_cols], g_s.at[core], loc.at[1]),
    ]
    for copy in own:
        copy.start()

    dkv[...] = jnp.zeros_like(dkv)
    acc[...] = jnp.zeros_like(acc)
    m8[...] = jnp.full_like(m8, -1e30)
    l8[...] = jnp.zeros_like(l8)
    d8[...] = jnp.zeros_like(d8)

    for i in range(2):
        for s in range(2):
            pltpu.make_async_copy(k_in, kv.at[i, s, y, z], a_recv.at[i, s]).wait()

    def one(h, yy, zz, first):
        return kv.at[:, h, yy, zz] if first else (kv.at[:, 0, :, zz] if h == 0 else kv.at[:, 1, yy, :])

    def part(i, h, yy, zz, first):
        return kv.at[i, h, yy, zz] if first else (kv.at[i, 0, :, zz] if h == 0 else kv.at[i, 1, yy, :])

    sent = []
    for stage in range(2):
        steps = []
        for h in range(2):
            along_y = (h == 0) == (stage == 0)
            up, dn = ring[0] if along_y else ring[1]
            here = one(h, y, z, stage == 0)
            steps.append(remote(here, here, ag_send.at[stage, h, 0], ag_recv.at[stage, h, 0], up))
            steps.append(remote(here, here, ag_send.at[stage, h, 1], ag_recv.at[stage, h, 1], dn))
        for copy in steps:
            copy.start()
        for copy in steps:
            copy.wait_recv()
        more = []
        for h in range(2):
            along_y = (h == 0) == (stage == 0)
            up, dn = ring[0] if along_y else ring[1]
            if along_y:
                low, high = part(0, h, (y + 3) % 4, z, stage == 0), part(1, h, (y + 1) % 4, z, stage == 0)
            else:
                low, high = part(0, h, y, (z + 3) % 4, stage == 0), part(1, h, y, (z + 1) % 4, stage == 0)
            more.append(remote(low, low, ag_send.at[stage, h, 2], ag_recv.at[stage, h, 2], up))
            more.append(remote(high, high, ag_send.at[stage, h, 3], ag_recv.at[stage, h, 3], dn))
        for copy in more:
            copy.start()
        for copy in more:
            copy.wait_recv()
        sent += steps + more

    for copy in own:
        copy.wait()
    for copy in ex:
        copy.wait_recv()

    def tile2(ref, i):
        s, n = i // 4, i % 4
        return jnp.concatenate(
            [ref[s, :, lanes(n * 256, 128)], ref[s, :, lanes(n * 256 + 128, 128)]], axis=0
        )

    def prep(i, carry):
        cols = lanes(i * 256, 256)
        q_t[:, cols] = tile2(q_s, i).T
        g_t[:, cols] = tile2(g_s, i).T
        return carry

    lax.fori_loop(0, 16, prep, 0)

    def keys(i, kc):
        return kv[i, kc // 8, (kc // 2) % 4, pl.ds(2 * (kc % 2), 2)].reshape(CH, DH)

    def prep_k(kc, carry):
        k_t[:, lanes(kc * CH, CH)] = keys(0, kc).T
        return carry

    lax.fori_loop(0, 16, prep_k, 0)

    def visible(pos, kc):
        key_pos = kc * CH + lax.broadcasted_iota(jnp.int32, (CH, 256), 0)
        query_pos = pos * TOK + (lax.broadcasted_iota(jnp.int32, (CH, 256), 1) & 127)
        return key_pos <= query_pos

    def stats(pos, kc, i, masked):
        cols = lanes(i * 256, 256)
        s = dot(keys(0, kc), q_t[:, cols])
        dp = dot(keys(1, kc), g_t[:, cols])
        if masked:
            s = jnp.where(visible(pos, kc), s, -1e30)
        s = s.reshape(CH // 8, 8, 256)
        dp = dp.reshape(CH // 8, 8, 256)
        old = m8[:, cols]
        new = jnp.maximum(old, jnp.max(s, axis=0))
        w = jnp.exp2((s - new) * EXPO)
        shrink = jnp.exp2((old - new) * EXPO)
        m8[:, cols] = new
        l8[:, cols] = l8[:, cols] * shrink + jnp.sum(w, axis=0)
        d8[:, cols] = d8[:, cols] * shrink + jnp.sum(w * dp, axis=0)

    def grads(pos, kc, i, masked):
        cols = lanes(i * 256, 256)
        at = (kc // 8, (kc // 2) % 4, pl.ds(2 * (kc % 2), 2))
        s = dot(keys(0, kc), q_t[:, cols])
        dp = dot(keys(1, kc), g_t[:, cols])
        p = jnp.exp2(s * EXPO - top[:, cols])
        if masked:
            p = jnp.where(visible(pos, kc), p, 0.0)
        ds = p * (dp - rdot[:, cols])
        p_low, ds_low = p.astype(bf16), ds.astype(bf16)
        dkv[(1,) + at] += dot(p_low, tile2(g_s, i)).reshape(2, 128, 128)
        dkv[(0,) + at] += dot(ds_low, tile2(q_s, i)).reshape(2, 128, 128)
        acc[:, cols] += dot(k_t[:, lanes(kc * CH, CH)], ds_low)

    positions = (seq, 31 - seq)

    def sweep(fn):
        for blk in range(2):
            pos = positions[blk]

            def chunk(kc, carry, masked=False, pos=pos, blk=blk):
                for i in range(8):
                    fn(pos, kc, blk * 8 + i, masked)
                return carry

            lax.fori_loop(0, pos // 2, chunk, 0)
            chunk(pos // 2, 0, True)

    sweep(stats)
    high = jnp.max(m8[...], axis=0, keepdims=True)
    fold = jnp.exp2((m8[...] - high) * EXPO)
    total = jnp.sum(l8[...] * fold, axis=0, keepdims=True)
    top[...] = high * EXPO + jnp.log2(total)
    rdot[...] = jnp.sum(d8[...] * fold, axis=0, keepdims=True) / total
    sweep(grads)

    def finish(i, carry):
        s, n = i // 4, i % 4
        t = (acc[:, lanes(i * 256, 256)] * SCALE).T.astype(bf16)
        dq_s[s, :, lanes(n * 256, 128)] = t[:128]
        dq_s[s, :, lanes(n * 256 + 128, 128)] = t[128:]
        return carry

    lax.fori_loop(0, 16, finish, 0)

    back = []
    for n, (c_t, flip) in enumerate(((1 - core, 0), (core, 1), (1 - core, 1))):
        back.append(remote(
            dq_s.at[2 * flip + c_t], dq_out.at[:, own_cols], dq_send.at[n], dq_recv.at[n], mates[n]
        ))
    for copy in back:
        copy.start()
    mine = pltpu.make_async_copy(dq_s.at[core], dq_out.at[:, own_cols], loc.at[2])
    mine.start()

    def part_of(h, i, d):
        return dkv[i, 0, :, d] if h == 0 else dkv[i, 1, d, :]

    spots = (z, y)
    rings = ((z_up, z_dn), (y_up, y_dn))
    first = []
    for h in range(2):
        spot, (up, dn) = spots[h], rings[h]
        far = (spot + 2) % 4
        st1[h, 0] = part_of(h, 0, far).astype(bf16)
        st1[h, 1] = part_of(h, 1, far).astype(bf16)
        first.append(remote(st1.at[h, 0], rc1.at[h, 0], rs_send.at[0, h, 0], rs_recv.at[0, h, 0], dn))
        first.append(remote(st1.at[h, 1], rc1.at[h, 1], rs_send.at[0, h, 1], rs_recv.at[0, h, 1], up))
        first[-2].start()
        first[-1].start()
    for h in range(2):
        spot = spots[h]
        st2[h, 0, 1] = part_of(h, 1, (spot + 3) % 4).astype(bf16)
        st2[h, 1, 0] = part_of(h, 0, (spot + 1) % 4).astype(bf16)
    second = []
    for h in range(2):
        spot, (up, dn) = spots[h], rings[h]
        first[2 * h].wait_recv()
        st2[h, 0, 0] = (part_of(h, 0, (spot + 3) % 4) + rc1[h, 0].astype(f32)).astype(bf16)
        second.append(remote(st2.at[h, 0], rc2.at[h, 0], rs_send.at[1, h, 0], rs_recv.at[1, h, 0], dn))
        second[-1].start()
        first[2 * h + 1].wait_recv()
        st2[h, 1, 1] = (part_of(h, 1, (spot + 1) % 4) + rc1[h, 1].astype(f32)).astype(bf16)
        second.append(remote(st2.at[h, 1], rc2.at[h, 1], rs_send.at[1, h, 1], rs_recv.at[1, h, 1], up))
        second[-1].start()
    for h in range(2):
        second[2 * h].wait_recv()
        second[2 * h + 1].wait_recv()
        for i in range(2):
            red[h, i] = part_of(h, i, spots[h]) + rc2[h, 0, i].astype(f32) + rc2[h, 1, i].astype(f32)

    third, fourth = [], []
    for h in range(2):
        spot, (up, dn) = spots[1 - h], rings[1 - h]
        far = (spot + 2) % 4
        st3[h, 0] = red[h, 0, far]
        st3[h, 1] = red[h, 1, far]
        third.append(remote(st3.at[h, 0], rc3.at[h, 0], rs_send.at[2, h, 0], rs_recv.at[2, h, 0], dn))
        third.append(remote(st3.at[h, 1], rc3.at[h, 1], rs_send.at[2, h, 1], rs_recv.at[2, h, 1], up))
        third[-2].start()
        third[-1].start()
        st4[h, 0, 1] = red[h, 1, (spot + 3) % 4]
        st4[h, 1, 0] = red[h, 0, (spot + 1) % 4]
    for h in range(2):
        spot, (up, dn) = spots[1 - h], rings[1 - h]
        third[2 * h].wait_recv()
        st4[h, 0, 0] = red[h, 0, (spot + 3) % 4] + rc3[h, 0]
        fourth.append(remote(st4.at[h, 0], rc4.at[h, 0], rs_send.at[3, h, 0], rs_recv.at[3, h, 0], dn))
        fourth[-1].start()
        third[2 * h + 1].wait_recv()
        st4[h, 1, 1] = red[h, 1, (spot + 1) % 4] + rc3[h, 1]
        fourth.append(remote(st4.at[h, 1], rc4.at[h, 1], rs_send.at[3, h, 1], rs_recv.at[3, h, 1], up))
        fourth[-1].start()

    def x_copies(h):
        to_self = jnp.logical_and(x_hi == x_lo, h == x_lo)
        local = pltpu.make_async_copy(fin.at[h], rcx.at[x_hi], x_recv.at[x_hi])
        away = remote(fin.at[h], rcx.at[x_hi], x_send.at[h], x_recv.at[x_hi], x_from(h))
        return to_self, local, away

    for h in range(2):
        fourth[2 * h].wait_recv()
        fourth[2 * h + 1].wait_recv()
        for i in range(2):
            fin[h, i] = red[h, i, spots[1 - h]] + rc4[h, 0, i] + rc4[h, 1, i]
        to_self, local, away = x_copies(h)

        @pl.when(to_self)
        def _(local=local):
            local.start()

        @pl.when(jnp.logical_not(to_self))
        def _(away=away):
            away.start()

    for s in range(2):
        pltpu.make_async_copy(fin.at[0], rcx.at[s], x_recv.at[s]).wait()
    dk_out[...] = ((rcx[0, 0] + rcx[1, 0]) * SCALE).astype(bf16)
    dv_out[...] = (rcx[0, 1] + rcx[1, 1]).astype(bf16)

    mine.wait()
    for copy in back:
        copy.wait()
    for copy in ex + sent + first + second + third + fourth:
        copy.wait_send()
    for t in range(2):
        to_self, pairs = a_copies(t)
        for _, away in pairs:
            @pl.when(jnp.logical_not(to_self))
            def _(away=away):
                away.wait_send()

        to_self, _, away = x_copies(t)

        @pl.when(jnp.logical_not(to_self))
        def _(away=away):
            away.wait_send()


def body(queries, shared_keys, shared_values, out_grad):
    any_, vmem = pl.BlockSpec(memory_space=pl.ANY), pl.BlockSpec(memory_space=pltpu.VMEM)
    dma = pltpu.SemaphoreType.DMA
    big, small = (2, 2, 4, 128, 128), (2, 2, 2, 128, 128)
    dq, dk, dv = pl.pallas_call(
        kernel,
        out_shape=(
            jax.ShapeDtypeStruct((128, 4096), bf16),
            jax.ShapeDtypeStruct((128, 128), bf16),
            jax.ShapeDtypeStruct((128, 128), bf16),
        ),
        in_specs=[any_] * 4,
        out_specs=(any_, vmem, vmem),
        scratch_shapes=[
            pltpu.VMEM((4, 128, 1024), bf16),
            pltpu.VMEM((4, 128, 1024), bf16),
            pltpu.VMEM((4, 128, 1024), bf16),
            pltpu.VMEM((2, 2, 4, 4, 128, 128), bf16),
            pltpu.VMEM((128, 4096), bf16),
            pltpu.VMEM((128, 4096), bf16),
            pltpu.VMEM((128, 4096), bf16),
            pltpu.VMEM((128, 4096), f32),
            pltpu.VMEM((2, 2, 4, 4, 128, 128), f32),
            pltpu.VMEM((8, 4096), f32),
            pltpu.VMEM((8, 4096), f32),
            pltpu.VMEM((8, 4096), f32),
            pltpu.VMEM((1, 4096), f32),
            pltpu.VMEM((1, 4096), f32),
            pltpu.VMEM(big, bf16),
            pltpu.VMEM(big, bf16),
            pltpu.VMEM((2,) + big, bf16),
            pltpu.VMEM((2,) + big, bf16),
            pltpu.VMEM(big, f32),
            pltpu.VMEM((2, 2, 128, 128), f32),
            pltpu.VMEM((2, 2, 128, 128), f32),
            pltpu.VMEM(small, f32),
            pltpu.VMEM(small, f32),
            pltpu.VMEM((2, 2, 128, 128), f32),
            pltpu.VMEM((2, 2, 128, 128), f32),
            dma((2, 3)), dma((2, 3)), dma((3,)),
            dma((2, 2)), dma((2, 2)),
            dma((2, 2, 4)), dma((2, 2, 4)),
            dma((4, 2, 2)), dma((4, 2, 2)),
            dma((2,)), dma((2,)),
            dma((3,)), dma((3,)),
        ],
        compiler_params=pltpu.CompilerParams(
            collective_id=0, has_side_effects=True, vmem_limit_bytes=56 * 2**20
        ),
        cost_estimate=pl.CostEstimate(flops=16 * 10**9, bytes_accessed=4 * 2**20, transcendentals=18 * 10**6),
    )(queries[0], shared_keys, shared_values, out_grad[0])
    return dq[None], dk, dv


def solution(mesh):
    return jax.shard_map(
        body,
        mesh=mesh,
        in_specs=(P("pipe", "seq", None), P("seq", "pipe"), P("seq", "pipe"), P("pipe", "seq", None)),
        out_specs=(P("pipe", "seq", None), P("seq", "pipe"), P("seq", "pipe")),
        check_vma=False,
    )
```

time: 975 us -> 148 us (0.15)
  the two profiles are of different devices: /device:TPU:1 before, /device:TPU:0 now
where the time goes in v1:
time: 148 us; the launch traced here: 147 us
  Pallas kernels  143 us (97%)
  local copies, waits for them, and re-layouts  3.68 us (2%)
    pallas_call x1, Pallas kernels, body(): pl.pallas_call(kernel, out_shape=(jax.ShapeDtypeStruct((128, 4096), bf16)...  143 us
    unnamed x7, local copies, waits for them, and re-layouts  3.68 us

profile of v1, /device:TPU:0, one launch (start us, length us, event | category | flops | bytes accessed | tf_op | source)
XLA Modules:
  0.0 147.4 jit_solution(11416181669638388188)
XLA Ops:
  0.6 143.1 %shard_map.67 = (bf16[128,4096]{1,0:T(8,128)(2,1)}, bf16[128,128]{1,0:T(8,128)(2,1)}, bf16[128,128]{1,0:T(8,128)(2,1)}) custom-call(bf16[128,4096]{1,0:T(8,128)(2,1)} %bitcast.4, bf16[128,128]{1,0:T(8,128)(2,1)} %k_in.1, bf16[128,128]{1,0:T(8,128)(2,1)} %v_in.1, bf16[128,4096]{1,0:T(8,128)(2,1)} %bitcast.5), custom_call_target="tpu_custom_call" | custom-call | flops 16000000000 | bytes 4194304 | tf_op jit(solution)/shard_map/pallas_call | solution.py:383
  143.7 0.0 copy-start.1
  143.7 2.3 %copy.10 = bf16[1,128,4096]{2,1,0:T(8,128)(2,1)} copy(bf16[1,128,4096]{2,1,0:T(8,128)(2,1)} %bitcast.3) | data formatting | bytes 2097152
  146.0 0.0 copy-done.1
  146.0 0.0 copy-start
  146.0 0.6 copy.11
  146.6 0.2 copy-done
  146.8 0.6 copy.12
Async XLA Ops:
  143.7 2.3 %copy-start.1 = (bf16[128,128]{1,0:T(8,128)(2,1)S(1)}, bf16[128,128]{1,0:T(8,128)(2,1)}, u32[]{:S(2)}) copy-start(bf16[128,128]{1,0:T(8,128)(2,1)} %get-tuple-element.13) | copy-start | bytes 98308
  146.0 0.8 copy-start

commit v2 on v1

--- a/solution.py
+++ b/solution.py
@@ -76,6 +76,40 @@
         def _():
             pl.semaphore_signal(barrier, inc=1, device_id=x_from(t), device_id_type=pl.DeviceIdType.MESH)
 
+    own_cols = lanes(head * 1024, 1024)
+    own = [
+        pltpu.make_async_copy(q_in.at[:, own_cols], q_s.at[core], loc.at[0]),
+        pltpu.make_async_copy(g_in.at[:, own_cols], g_s.at[core], loc.at[1]),
+    ]
+    for copy in own:
+        copy.start()
+
+    def clear(i, carry):
+        dkv[i // 8, (i // 4) % 2, i % 4] = jnp.zeros((4, 128, 128), f32)
+        return carry
+
+    lax.fori_loop(0, 16, clear, 0)
+    acc[...] = jnp.zeros_like(acc)
+    m8[...] = jnp.full_like(m8, -1e30)
+    l8[...] = jnp.zeros_like(l8)
+    d8[...] = jnp.zeros_like(d8)
+
+    def tile2(ref, i):
+        s, n = i // 4, i % 4
+        return jnp.concatenate(
+            [ref[s, :, lanes(n * 256, 128)], ref[s, :, lanes(n * 256 + 128, 128)]], axis=0
+        )
+
+    def prep(i, carry=0):
+        cols = lanes(i * 256, 256)
+        q_t[:, cols] = tile2(q_s, i).T
+        g_t[:, cols] = tile2(g_s, i).T
+        return carry
+
+    for copy in own:
+        copy.wait()
+    lax.fori_loop(0, 4, lambda n, carry: prep(core * 4 + n), 0)
+
     @pl.when(x_hi == x_lo)
     def _():
         pl.semaphore_wait(barrier, 9)
@@ -106,28 +140,21 @@
             def _(away=away):
                 away.start()
 
-    ex = []
-    for n, (c_t, flip) in enumerate(((1 - core, 0), (core, 1), (1 - core, 1))):
+    def exchange(n, half):
+        c_t, flip = ((1 - core, 0), (core, 1), (1 - core, 1))[n]
         x_t = (1 - x_lo) if flip else x_lo
-        cols = lanes((2 * x_t + c_t) * 1024, 1024)
+        cols = lanes((2 * x_t + c_t) * 1024 + half * 512, 512)
+        there = lanes(half * 512, 512)
         slot = 2 * flip + core
-        for i, (src, dst) in enumerate(((q_in, q_s), (g_in, g_s))):
-            ex.append(remote(src.at[:, cols], dst.at[slot], ex_send.at[i, n], ex_recv.at[i, n], mates[n]))
-    for copy in ex:
-        copy.start()
-    own_cols = lanes(head * 1024, 1024)
-    own = [
-        pltpu.make_async_copy(q_in.at[:, own_cols], q_s.at[core], loc.at[0]),
-        pltpu.make_async_copy(g_in.at[:, own_cols], g_s.at[core], loc.at[1]),
-    ]
-    for copy in own:
-        copy.start()
-
-    dkv[...] = jnp.zeros_like(dkv)
-    acc[...] = jnp.zeros_like(acc)
-    m8[...] = jnp.full_like(m8, -1e30)
-    l8[...] = jnp.zeros_like(l8)
-    d8[...] = jnp.zeros_like(d8)
+        return [
+            remote(src.at[:, cols], dst.at[slot, :, there], ex_send.at[i, n, half], ex_recv.at[i, n, half], mates[n])
+            for i, (src, dst) in enumerate(((q_in, q_s), (g_in, g_s)))
+        ]
+
+    ex = [[exchange(n, half) for half in range(2)] for n in range(3)]
+    for half in range(2):
+        for copy in ex[0][half]:
+            copy.start()
 
     for i in range(2):
         for s in range(2):
@@ -139,8 +166,7 @@
     def part(i, h, yy, zz, first):
         return kv.at[i, h, yy, zz] if first else (kv.at[i, 0, :, zz] if h == 0 else kv.at[i, 1, yy, :])
 
-    sent = []
-    for stage in range(2):
+    def near(stage):
         steps = []
         for h in range(2):
             along_y = (h == 0) == (stage == 0)
@@ -148,11 +174,10 @@
             here = one(h, y, z, stage == 0)
             steps.append(remote(here, here, ag_send.at[stage, h, 0], ag_recv.at[stage, h, 0], up))
             steps.append(remote(here, here, ag_send.at[stage, h, 1], ag_recv.at[stage, h, 1], dn))
-        for copy in steps:
-            copy.start()
-        for copy in steps:
-            copy.wait_recv()
-        more = []
+        return steps
+
+    def onward(stage):
+        steps = []
         for h in range(2):
             along_y = (h == 0) == (stage == 0)
             up, dn = ring[0] if along_y else ring[1]
@@ -160,41 +185,34 @@
                 low, high = part(0, h, (y + 3) % 4, z, stage == 0), part(1, h, (y + 1) % 4, z, stage == 0)
             else:
                 low, high = part(0, h, y, (z + 3) % 4, stage == 0), part(1, h, y, (z + 1) % 4, stage == 0)
-            more.append(remote(low, low, ag_send.at[stage, h, 2], ag_recv.at[stage, h, 2], up))
-            more.append(remote(high, high, ag_send.at[stage, h, 3], ag_recv.at[stage, h, 3], dn))
-        for copy in more:
+            steps.append(remote(low, low, ag_send.at[stage, h, 2], ag_recv.at[stage, h, 2], up))
+            steps.append(remote(high, high, ag_send.at[stage, h, 3], ag_recv.at[stage, h, 3], dn))
+        return steps
+
+    near0, onward0, near1, onward1 = near(0), onward(0), near(1), onward(1)
+    for copy in near0:
+        copy.start()
+    for n in (1, 2):
+        for copy in ex[n][0]:
             copy.start()
-        for copy in more:
+    for copy in near0:
+        copy.wait_recv()
+    for copy in onward0:
+        copy.start()
+    for half in range(2):
+        for copy in ex[0][half]:
             copy.wait_recv()
-        sent += steps + more
-
-    for copy in own:
-        copy.wait()
-    for copy in ex:
+    lax.fori_loop(0, 4, lambda n, carry: prep((1 - core) * 4 + n), 0)
+    for copy in onward0:
         copy.wait_recv()
-
-    def tile2(ref, i):
-        s, n = i // 4, i % 4
-        return jnp.concatenate(
-            [ref[s, :, lanes(n * 256, 128)], ref[s, :, lanes(n * 256 + 128, 128)]], axis=0
-        )
-
-    def prep(i, carry):
-        cols = lanes(i * 256, 256)
-        q_t[:, cols] = tile2(q_s, i).T
-        g_t[:, cols] = tile2(g_s, i).T
-        return carry
-
-    lax.fori_loop(0, 16, prep, 0)
+    for copy in near1:
+        copy.start()
+    for n in (1, 2):
+        for copy in ex[n][1]:
+            copy.start()
 
     def keys(i, kc):
         return kv[i, kc // 8, (kc // 2) % 4, pl.ds(2 * (kc % 2), 2)].reshape(CH, DH)
-
-    def prep_k(kc, carry):
-        k_t[:, lanes(kc * CH, CH)] = keys(0, kc).T
-        return carry
-
-    lax.fori_loop(0, 16, prep_k, 0)
 
     def visible(pos, kc):
         key_pos = kc * CH + lax.broadcasted_iota(jnp.int32, (CH, 256), 0)
@@ -233,103 +251,132 @@
 
     positions = (seq, 31 - seq)
 
-    def sweep(fn):
-        for blk in range(2):
-            pos = positions[blk]
-
-            def chunk(kc, carry, masked=False, pos=pos, blk=blk):
-                for i in range(8):
-                    fn(pos, kc, blk * 8 + i, masked)
-                return carry
-
-            lax.fori_loop(0, pos // 2, chunk, 0)
-            chunk(pos // 2, 0, True)
-
-    sweep(stats)
+    def chunk(fn, blk, kc, tiles):
+        pos = positions[blk]
+
+        @pl.when(kc < pos // 2)
+        def _():
+            for i in tiles:
+                fn(pos, kc, i, False)
+
+        @pl.when(kc == pos // 2)
+        def _():
+            for i in tiles:
+                fn(pos, kc, i, True)
+
+    def near_rows(o, carry):
+        @pl.when(o == 2)
+        def _():
+            for copy in near1:
+                copy.wait_recv()
+            for copy in onward1:
+                copy.start()
+
+        @pl.when(o == 6)
+        def _():
+            for copy in onward1:
+                copy.wait_recv()
+
+        late, r = o // 8, o // 2
+        turn = r + r // 2 - 2 * (r // 3)
+        kc = (1 - late) * (8 + ((y + turn) % 4) * 2 + o % 2) + late * (o - 8)
+        chunk(stats, 0, kc, range(8))
+        return carry
+
+    lax.fori_loop(0, 16, near_rows, 0)
+
+    def far_rows(half, carry):
+        for n in (1, 2):
+            for i in range(2):
+                pltpu.make_async_copy(
+                    q_s.at[0, :, lanes(0, 512)], q_s.at[0, :, lanes(0, 512)], ex_recv.at[i, n, half]
+                ).wait()
+        tiles = [8 + 2 * half, 9 + 2 * half, 12 + 2 * half, 13 + 2 * half]
+        for i in tiles:
+            prep(i)
+        pos = positions[1]
+
+        def full(kc, carry):
+            for i in tiles:
+                stats(pos, kc, i, False)
+            return carry
+
+        lax.fori_loop(0, pos // 2, full, 0)
+        for i in tiles:
+            stats(pos, pos // 2, i, True)
+        return carry
+
+    lax.fori_loop(0, 2, far_rows, 0)
+
+    def prep_k(kc, carry):
+        k_t[:, lanes(kc * CH, CH)] = keys(0, kc).T
+        return carry
+
+    lax.fori_loop(0, 16, prep_k, 0)
     high = jnp.max(m8[...], axis=0, keepdims=True)
     fold = jnp.exp2((m8[...] - high) * EXPO)
     total = jnp.sum(l8[...] * fold, axis=0, keepdims=True)
     top[...] = high * EXPO + jnp.log2(total)
     rdot[...] = jnp.sum(d8[...] * fold, axis=0, keepdims=True) / total
-    sweep(grads)
-
-    def finish(i, carry):
-        s, n = i // 4, i % 4
-        t = (acc[:, lanes(i * 256, 256)] * SCALE).T.astype(bf16)
-        dq_s[s, :, lanes(n * 256, 128)] = t[:128]
-        dq_s[s, :, lanes(n * 256 + 128, 128)] = t[128:]
-        return carry
-
-    lax.fori_loop(0, 16, finish, 0)
-
-    back = []
-    for n, (c_t, flip) in enumerate(((1 - core, 0), (core, 1), (1 - core, 1))):
-        back.append(remote(
-            dq_s.at[2 * flip + c_t], dq_out.at[:, own_cols], dq_send.at[n], dq_recv.at[n], mates[n]
-        ))
-    for copy in back:
-        copy.start()
-    mine = pltpu.make_async_copy(dq_s.at[core], dq_out.at[:, own_cols], loc.at[2])
-    mine.start()
 
     def part_of(h, i, d):
         return dkv[i, 0, :, d] if h == 0 else dkv[i, 1, d, :]
 
     spots = (z, y)
     rings = ((z_up, z_dn), (y_up, y_dn))
-    first = []
+    first, second, third, fourth = [], [], [], []
     for h in range(2):
-        spot, (up, dn) = spots[h], rings[h]
-        far = (spot + 2) % 4
-        st1[h, 0] = part_of(h, 0, far).astype(bf16)
-        st1[h, 1] = part_of(h, 1, far).astype(bf16)
+        up, dn = rings[h]
         first.append(remote(st1.at[h, 0], rc1.at[h, 0], rs_send.at[0, h, 0], rs_recv.at[0, h, 0], dn))
         first.append(remote(st1.at[h, 1], rc1.at[h, 1], rs_send.at[0, h, 1], rs_recv.at[0, h, 1], up))
-        first[-2].start()
-        first[-1].start()
-    for h in range(2):
+        second.append(remote(st2.at[h, 0], rc2.at[h, 0], rs_send.at[1, h, 0], rs_recv.at[1, h, 0], dn))
+        second.append(remote(st2.at[h, 1], rc2.at[h, 1], rs_send.at[1, h, 1], rs_recv.at[1, h, 1], up))
+        up, dn = rings[1 - h]
+        third.append(remote(st3.at[h, 0], rc3.at[h, 0], rs_send.at[2, h, 0], rs_recv.at[2, h, 0], dn))
+        third.append(remote(st3.at[h, 1], rc3.at[h, 1], rs_send.at[2, h, 1], rs_recv.at[2, h, 1], up))
+        fourth.append(remote(st4.at[h, 0], rc4.at[h, 0], rs_send.at[3, h, 0], rs_recv.at[3, h, 0], dn))
+        fourth.append(remote(st4.at[h, 1], rc4.at[h, 1], rs_send.at[3, h, 1], rs_recv.at[3, h, 1], up))
+
+    def reduce1(h):
+        far = (spots[h] + 2) % 4
+        st1[h, 0] = part_of(h, 0, far).astype(bf16)
+        first[2 * h].start()
+        st1[h, 1] = part_of(h, 1, far).astype(bf16)
+        first[2 * h + 1].start()
+
+    def reduce2(h):
         spot = spots[h]
         st2[h, 0, 1] = part_of(h, 1, (spot + 3) % 4).astype(bf16)
         st2[h, 1, 0] = part_of(h, 0, (spot + 1) % 4).astype(bf16)
-    second = []
-    for h in range(2):
-        spot, (up, dn) = spots[h], rings[h]
         first[2 * h].wait_recv()
         st2[h, 0, 0] = (part_of(h, 0, (spot + 3) % 4) + rc1[h, 0].astype(f32)).astype(bf16)
-        second.append(remote(st2.at[h, 0], rc2.at[h, 0], rs_send.at[1, h, 0], rs_recv.at[1, h, 0], dn))
-        second[-1].start()
+        second[2 * h].start()
         first[2 * h + 1].wait_recv()
         st2[h, 1, 1] = (part_of(h, 1, (spot + 1) % 4) + rc1[h, 1].astype(f32)).astype(bf16)
-        second.append(remote(st2.at[h, 1], rc2.at[h, 1], rs_send.at[1, h, 1], rs_recv.at[1, h, 1], up))
-        second[-1].start()
-    for h in range(2):
+        second[2 * h + 1].start()
+
+    def reduce3(h):
         second[2 * h].wait_recv()
         second[2 * h + 1].wait_recv()
         for i in range(2):
             red[h, i] = part_of(h, i, spots[h]) + rc2[h, 0, i].astype(f32) + rc2[h, 1, i].astype(f32)
-
-    third, fourth = [], []
-    for h in range(2):
-        spot, (up, dn) = spots[1 - h], rings[1 - h]
+        spot = spots[1 - h]
         far = (spot + 2) % 4
         st3[h, 0] = red[h, 0, far]
+        third[2 * h].start()
         st3[h, 1] = red[h, 1, far]
-        third.append(remote(st3.at[h, 0], rc3.at[h, 0], rs_send.at[2, h, 0], rs_recv.at[2, h, 0], dn))
-        third.append(remote(st3.at[h, 1], rc3.at[h, 1], rs_send.at[2, h, 1], rs_recv.at[2, h, 1], up))
-        third[-2].start()
-        third[-1].start()
+        third[2 * h + 1].start()
         st4[h, 0, 1] = red[h, 1, (spot + 3) % 4]
         st4[h, 1, 0] = red[h, 0, (spot + 1) % 4]
-    for h in range(2):
-        spot, (up, dn) = spots[1 - h], rings[1 - h]
+
+    def reduce4(h):
+        spot = spots[1 - h]
         third[2 * h].wait_recv()
         st4[h, 0, 0] = red[h, 0, (spot + 3) % 4] + rc3[h, 0]
-        fourth.append(remote(st4.at[h, 0], rc4.at[h, 0], rs_send.at[3, h, 0], rs_recv.at[3, h, 0], dn))
-        fourth[-1].start()
+        fourth[2 * h].start()
         third[2 * h + 1].wait_recv()
         st4[h, 1, 1] = red[h, 1, (spot + 1) % 4] + rc3[h, 1]
-        fourth.append(remote(st4.at[h, 1], rc4.at[h, 1], rs_send.at[3, h, 1], rs_recv.at[3, h, 1], up))
-        fourth[-1].start()
+        fourth[2 * h + 1].start()
 
     def x_copies(h):
         to_self = jnp.logical_and(x_hi == x_lo, h == x_lo)
@@ -337,7 +384,7 @@
         away = remote(fin.at[h], rcx.at[x_hi], x_send.at[h], x_recv.at[x_hi], x_from(h))
         return to_self, local, away
 
-    for h in range(2):
+    def reduce5(h):
         fourth[2 * h].wait_recv()
         fourth[2 * h + 1].wait_recv()
         for i in range(2):
@@ -345,12 +392,70 @@
         to_self, local, away = x_copies(h)
 
         @pl.when(to_self)
-        def _(local=local):
+        def _():
             local.start()
 
         @pl.when(jnp.logical_not(to_self))
-        def _(away=away):
+        def _():
             away.start()
+
+    def finish(layer):
+        for blk in range(2):
+            s = 2 * blk + layer
+            for n in range(4):
+                t = (acc[:, lanes((s * 4 + n) * 256, 256)] * SCALE).T.astype(bf16)
+                dq_s[s, :, lanes(n * 256, 128)] = t[:128]
+                dq_s[s, :, lanes(n * 256 + 128, 128)] = t[128:]
+
+    mine = pltpu.make_async_copy(dq_s.at[core], dq_out.at[:, own_cols], loc.at[2])
+    back = [
+        remote(dq_s.at[2 * flip + c_t], dq_out.at[:, own_cols], dq_send.at[n], dq_recv.at[n], mates[n])
+        for n, (c_t, flip) in enumerate(((1 - core, 0), (core, 1), (1 - core, 1)))
+    ]
+
+    def rows(sweep, carry):
+        layer = (core + 1 + sweep) % 2
+
+        def cell(o, carry):
+            for at, act in ((2, lambda: reduce1(1)), (6, lambda: reduce1(0)), (10, lambda: reduce2(1)), (12, lambda: reduce3(1))):
+                @pl.when(jnp.logical_and(sweep == 1, o == at))
+                def _(act=act):
+                    act()
+
+            kc = order(o)
+            for blk in range(2):
+                chunk(grads, blk, kc, [8 * blk + 4 * layer + n for n in range(4)])
+            return carry
+
+        lax.fori_loop(0, 16, cell, 0)
+        finish(layer)
+
+        @pl.when(sweep == 0)
+        def _():
+            back[0].start()
+            back[2].start()
+
+        return carry
+
+    def order(o):
+        pick = [
+            8 + ((y + 2) % 4) * 2 + o,
+            (o - 2) * 2 + 1 - z // 2,
+            8 + ((y + 1 + 2 * ((o - 6) // 2) - (o - 6) // 4) % 4) * 2 + o % 2,
+            (o - 12) * 2 + z // 2,
+        ]
+        g1, g2, g3 = (o + 14) // 16, (o + 10) // 16, (o + 4) // 16
+        return pick[0] * (1 - g1) + pick[1] * (g1 - g2) + pick[2] * (g2 - g3) + pick[3] * g3
+
+    lax.fori_loop(0, 2, rows, 0)
+    back[1].start()
+    mine.start()
+    reduce2(0)
+    reduce4(1)
+    reduce3(0)
+    reduce5(1)
+    reduce4(0)
+    reduce5(0)
 
     for s in range(2):
         pltpu.make_async_copy(fin.at[0], rcx.at[s], x_recv.at[s]).wait()
@@ -360,7 +465,7 @@
     mine.wait()
     for copy in back:
         copy.wait()
-    for copy in ex + sent + first + second + third + fourth:
+    for copy in sum(ex[0] + ex[1] + ex[2], []) + near0 + onward0 + near1 + onward1 + first + second + third + fourth:
         copy.wait_send()
     for t in range(2):
         to_self, pairs = a_copies(t)
@@ -415,7 +520,7 @@
             pltpu.VMEM(small, f32),
             pltpu.VMEM((2, 2, 128, 128), f32),
             pltpu.VMEM((2, 2, 128, 128), f32),
-            dma((2, 3)), dma((2, 3)), dma((3,)),
+            dma((2, 3, 2)), dma((2, 3, 2)), dma((3,)),
             dma((2, 2)), dma((2, 2)),
             dma((2, 2, 4)), dma((2, 2, 4)),
             dma((4, 2, 2)), dma((4, 2, 2)),

time: 148 us -> 150 us (1.014)
  the two profiles are of different devices: /device:TPU:0 before, /device:TPU:104 now
where the time goes in v2:
time: 150 us
  Pallas kernels  145 us (97%)
  local copies, waits for them, and re-layouts  3.68 us (2%)
    pallas_call x1, Pallas kernels, body(): pl.pallas_call(kernel, out_shape=(jax.ShapeDtypeStruct((128, 4096), bf16)...  145 us
    unnamed x7, local copies, waits for them, and re-layouts  3.68 us

profile of v2, /device:TPU:104, one launch (start us, length us, event | category | flops | bytes accessed | tf_op | source)
XLA Modules:
  0.0 149.5 jit_solution(6901086280135062206)
XLA Ops:
  0.6 145.2 %shard_map.67 = (bf16[128,4096]{1,0:T(8,128)(2,1)}, bf16[128,128]{1,0:T(8,128)(2,1)}, bf16[128,128]{1,0:T(8,128)(2,1)}) custom-call(bf16[128,4096]{1,0:T(8,128)(2,1)} %bitcast.4, bf16[128,128]{1,0:T(8,128)(2,1)} %k_in.1, bf16[128,128]{1,0:T(8,128)(2,1)} %v_in.1, bf16[128,4096]{1,0:T(8,128)(2,1)} %bitcast.5), custom_call_target="tpu_custom_call" | custom-call | flops 16000000000 | bytes 4194304 | tf_op jit(solution)/shard_map/pallas_call | solution.py:488
  145.8 0.0 copy-start.1
  145.9 2.3 %copy.10 = bf16[1,128,4096]{2,1,0:T(8,128)(2,1)} copy(bf16[1,128,4096]{2,1,0:T(8,128)(2,1)} %bitcast.3) | data formatting | bytes 2097152
  148.2 0.0 copy-done.1
  148.2 0.0 copy-start
  148.2 0.6 copy.11
  148.8 0.2 copy-done
  148.9 0.6 copy.12
Async XLA Ops:
  145.8 2.3 %copy-start.1 = (bf16[128,128]{1,0:T(8,128)(2,1)S(1)}, bf16[128,128]{1,0:T(8,128)(2,1)}, u32[]{:S(2)}) copy-start(bf16[128,128]{1,0:T(8,128)(2,1)} %get-tuple-element.13) | copy-start | bytes 98308
  148.2 0.8 copy-start

commit v3 on v2

--- a/solution.py
+++ b/solution.py
@@ -31,7 +31,7 @@
     q_s, g_s, dq_s, kv, q_t, g_t, k_t, acc, dkv,
     m8, l8, d8, top, rdot,
     st1, rc1, st2, rc2, red, st3, rc3, st4, rc4, fin, rcx,
-    ex_send, ex_recv, loc, a_send, a_recv, ag_send, ag_recv,
+    ex_send, ex_recv, loc, a_send, a_recv, clear_sem, y_send, y_recv, z_send, z_recv,
     rs_send, rs_recv, x_send, x_recv, dq_send, dq_recv,
 ):
     pipe = lax.axis_index("pipe")
@@ -51,12 +51,15 @@
 
     mates = [
         dev(x_hi, 1 - core, x_lo, y, z),
-        dev(x_hi, core, 1 - x_lo, 3 - y, 3 - z),
-        dev(x_hi, 1 - core, 1 - x_lo, 3 - y, 3 - z),
+        dev(x_hi, core, 1 - x_lo, 3 - y, z),
+        dev(x_hi, 1 - core, 1 - x_lo, 3 - y, z),
     ]
     y_up, y_dn = dev(x_hi, core, x_lo, (y + 1) % 4, z), dev(x_hi, core, x_lo, (y + 3) % 4, z)
     z_up, z_dn = dev(x_hi, core, x_lo, y, (z + 1) % 4), dev(x_hi, core, x_lo, y, (z + 3) % 4)
-    ring = ((y_up, y_dn), (z_up, z_dn))
+    y_step = 1 - 2 * (y % 2)
+    y_all = (dev(x_hi, core, x_lo, 3 - y, z), dev(x_hi, core, x_lo, y + y_step, z))
+    gate = [mates[0], dev(x_hi, core, 1 - x_lo, y, z), dev(x_hi, 1 - core, 1 - x_lo, y, z)]
+    z_all = (z_up, z_dn, dev(x_hi, core, x_lo, y, (z + 2) % 4))
 
     def x_to(t):
         return dev(t, core, x_hi, y, z)
@@ -65,7 +68,7 @@
         return dev(x_lo, core, s, y, z)
 
     barrier = pltpu.get_barrier_semaphore()
-    for peer in mates + [y_up, y_dn, z_up, z_dn]:
+    for peer in mates + list(y_all + z_all) + gate[1:]:
         pl.semaphore_signal(barrier, inc=1, device_id=peer, device_id_type=pl.DeviceIdType.MESH)
     for t in range(2):
         @pl.when(jnp.logical_not(jnp.logical_and(t == x_hi, x_lo == x_hi)))
@@ -112,11 +115,11 @@
 
     @pl.when(x_hi == x_lo)
     def _():
-        pl.semaphore_wait(barrier, 9)
+        pl.semaphore_wait(barrier, 12)
 
     @pl.when(x_hi != x_lo)
     def _():
-        pl.semaphore_wait(barrier, 11)
+        pl.semaphore_wait(barrier, 14)
 
     def a_copies(t):
         to_self = jnp.logical_and(t == x_hi, x_lo == x_hi)
@@ -160,56 +163,41 @@
         for s in range(2):
             pltpu.make_async_copy(k_in, kv.at[i, s, y, z], a_recv.at[i, s]).wait()
 
-    def one(h, yy, zz, first):
-        return kv.at[:, h, yy, zz] if first else (kv.at[:, 0, :, zz] if h == 0 else kv.at[:, 1, yy, :])
-
-    def part(i, h, yy, zz, first):
-        return kv.at[i, h, yy, zz] if first else (kv.at[i, 0, :, zz] if h == 0 else kv.at[i, 1, yy, :])
-
-    def near(stage):
-        steps = []
-        for h in range(2):
-            along_y = (h == 0) == (stage == 0)
-            up, dn = ring[0] if along_y else ring[1]
-            here = one(h, y, z, stage == 0)
-            steps.append(remote(here, here, ag_send.at[stage, h, 0], ag_recv.at[stage, h, 0], up))
-            steps.append(remote(here, here, ag_send.at[stage, h, 1], ag_recv.at[stage, h, 1], dn))
-        return steps
-
-    def onward(stage):
-        steps = []
-        for h in range(2):
-            along_y = (h == 0) == (stage == 0)
-            up, dn = ring[0] if along_y else ring[1]
-            if along_y:
-                low, high = part(0, h, (y + 3) % 4, z, stage == 0), part(1, h, (y + 1) % 4, z, stage == 0)
-            else:
-                low, high = part(0, h, y, (z + 3) % 4, stage == 0), part(1, h, y, (z + 1) % 4, stage == 0)
-            steps.append(remote(low, low, ag_send.at[stage, h, 2], ag_recv.at[stage, h, 2], up))
-            steps.append(remote(high, high, ag_send.at[stage, h, 3], ag_recv.at[stage, h, 3], dn))
-        return steps
-
-    near0, onward0, near1, onward1 = near(0), onward(0), near(1), onward(1)
-    for copy in near0:
+    def y_of(g):
+        base = y + (g // 2) * y_step
+        return base + (g % 2) * (3 - 2 * base)
+
+    def pair(g):
+        return kv.at[:, :, y_of(g), z]
+
+    y_copies = [
+        remote(pair(g), pair(g), y_send.at[d], y_recv.at[d], y_all[to]) for d, (g, to) in enumerate(((0, 0), (0, 1), (1, 1)))
+    ]
+    z_sent = [
+        [remote(pair(g), pair(g), z_send.at[g, d], z_recv.at[g, d], z_all[d]) for d in range(3)] for g in range(4)
+    ]
+    for copy in y_copies[:2] + z_sent[0]:
         copy.start()
-    for n in (1, 2):
-        for copy in ex[n][0]:
-            copy.start()
-    for copy in near0:
-        copy.wait_recv()
-    for copy in onward0:
+    y_copies[0].wait()
+    for peer in gate:
+        pl.semaphore_signal(clear_sem, inc=1, device_id=peer, device_id_type=pl.DeviceIdType.MESH)
+    for copy in [y_copies[2]] + z_sent[1]:
+        copy.start()
+    y_copies[1].wait_recv()
+    for copy in z_sent[2]:
+        copy.start()
+    pl.semaphore_wait(clear_sem, 3)
+    for half in range(2):
+        for n in (1, 2):
+            for copy in ex[n][half]:
+                copy.start()
+    y_copies[2].wait_recv()
+    for copy in z_sent[3]:
         copy.start()
     for half in range(2):
         for copy in ex[0][half]:
             copy.wait_recv()
     lax.fori_loop(0, 4, lambda n, carry: prep((1 - core) * 4 + n), 0)
-    for copy in onward0:
-        copy.wait_recv()
-    for copy in near1:
-        copy.start()
-    for n in (1, 2):
-        for copy in ex[n][1]:
-            copy.start()
 
     def keys(i, kc):
         return kv[i, kc // 8, (kc // 2) % 4, pl.ds(2 * (kc % 2), 2)].reshape(CH, DH)
@@ -235,21 +223,28 @@
         l8[:, cols] = l8[:, cols] * shrink + jnp.sum(w, axis=0)
         d8[:, cols] = d8[:, cols] * shrink + jnp.sum(w * dp, axis=0)
 
-    def grads(pos, kc, i, masked):
-        cols = lanes(i * 256, 256)
+    def tile8(ref, s):
+        return jnp.concatenate([ref[s, :, lanes(n * 128, 128)] for n in range(8)], axis=0)
+
+    def grads(pos, kc, s, masked):
         at = (kc // 8, (kc // 2) % 4, pl.ds(2 * (kc % 2), 2))
-        s = dot(keys(0, kc), q_t[:, cols])
-        dp = dot(keys(1, kc), g_t[:, cols])
-        p = jnp.exp2(s * EXPO - top[:, cols])
-        if masked:
-            p = jnp.where(visible(pos, kc), p, 0.0)
-        ds = p * (dp - rdot[:, cols])
-        p_low, ds_low = p.astype(bf16), ds.astype(bf16)
-        dkv[(1,) + at] += dot(p_low, tile2(g_s, i)).reshape(2, 128, 128)
-        dkv[(0,) + at] += dot(ds_low, tile2(q_s, i)).reshape(2, 128, 128)
-        acc[:, cols] += dot(k_t[:, lanes(kc * CH, CH)], ds_low)
-
-    positions = (seq, 31 - seq)
+        p_parts, ds_parts = [], []
+        for n in range(4):
+            cols = lanes(s * 1024 + n * 256, 256)
+            scores = dot(keys(0, kc), q_t[:, cols])
+            dp = dot(keys(1, kc), g_t[:, cols])
+            p = jnp.exp2(scores * EXPO - top[:, cols])
+            if masked:
+                p = jnp.where(visible(pos, kc), p, 0.0)
+            ds = p * (dp - rdot[:, cols])
+            p_parts.append(p.astype(bf16))
+            ds_parts.append(ds.astype(bf16))
+        p_low, ds_low = jnp.concatenate(p_parts, axis=1), jnp.concatenate(ds_parts, axis=1)
+        dkv[(1,) + at] += dot(p_low, tile8(g_s, s)).reshape(2, 128, 128)
+        dkv[(0,) + at] += dot(ds_low, tile8(q_s, s)).reshape(2, 128, 128)
+        acc[:, lanes(s * 1024, 1024)] += dot(k_t[:, lanes(kc * CH, CH)], ds_low)
+
+    positions = (seq, 16 * (1 - x_lo) + 4 * (3 - y) + z)
 
     def chunk(fn, blk, kc, tiles):
         pos = positions[blk]
@@ -264,55 +259,46 @@
             for i in tiles:
                 fn(pos, kc, i, True)
 
-    def near_rows(o, carry):
-        @pl.when(o == 2)
-        def _():
-            for copy in near1:
+    def far_tiles(half):
+        return [8 + 2 * half, 9 + 2 * half, 12 + 2 * half, 13 + 2 * half]
+
+    def far_arrive(half):
+        for n in (1, 2):
+            for copy in ex[n][half]:
                 copy.wait_recv()
-            for copy in onward1:
-                copy.start()
-
-        @pl.when(o == 6)
-        def _():
-            for copy in onward1:
-                copy.wait_recv()
-
-        late, r = o // 8, o // 2
-        turn = r + r // 2 - 2 * (r // 3)
-        kc = (1 - late) * (8 + ((y + turn) % 4) * 2 + o % 2) + late * (o - 8)
+        for i in far_tiles(half):
+            prep(i)
+
+    def first_rows(o, carry):
+        g = o // 4
+
+        @pl.when(o % 4 == 0)
+        def _():
+            for d in range(3):
+                pltpu.make_async_copy(kv.at[:, :, 0, 0], kv.at[:, :, 0, 0], z_recv.at[g, d]).wait()
+
+        @pl.when(o == 0)
+        def _():
+            far_arrive(0)
+
+        kc = ((o // 2) % 2) * 8 + y_of(g) * 2 + o % 2
+        k_t[:, lanes(kc * CH, CH)] = keys(0, kc).T
         chunk(stats, 0, kc, range(8))
+        chunk(stats, 1, kc, far_tiles(0))
         return carry
 
-    lax.fori_loop(0, 16, near_rows, 0)
-
-    def far_rows(half, carry):
-        for n in (1, 2):
-            for i in range(2):
-                pltpu.make_async_copy(
-                    q_s.at[0, :, lanes(0, 512)], q_s.at[0, :, lanes(0, 512)], ex_recv.at[i, n, half]
-                ).wait()
-        tiles = [8 + 2 * half, 9 + 2 * half, 12 + 2 * half, 13 + 2 * half]
-        for i in tiles:
-            prep(i)
-        pos = positions[1]
-
-        def full(kc, carry):
-            for i in tiles:
-                stats(pos, kc, i, False)
-            return carry
-
-        lax.fori_loop(0, pos // 2, full, 0)
-        for i in tiles:
-            stats(pos, pos // 2, i, True)
+    lax.fori_loop(0, 16, first_rows, 0)
+    far_arrive(1)
+
+    def last_rows(kc, carry):
+        for i in far_tiles(1):
+            stats(positions[1], kc, i, False)
         return carry
 
-    lax.fori_loop(0, 2, far_rows, 0)
-
-    def prep_k(kc, carry):
-        k_t[:, lanes(kc * CH, CH)] = keys(0, kc).T
-        return carry
-
-    lax.fori_loop(0, 16, prep_k, 0)
+    lax.fori_loop(0, positions[1] // 2, last_rows, 0)
+    for i in far_tiles(1):
+        stats(positions[1], positions[1] // 2, i, True)
+
     high = jnp.max(m8[...], axis=0, keepdims=True)
     fold = jnp.exp2((m8[...] - high) * EXPO)
     total = jnp.sum(l8[...] * fold, axis=0, keepdims=True)
@@ -417,17 +403,22 @@
         layer = (core + 1 + sweep) % 2
 
         def cell(o, carry):
-            for at, act in ((2, lambda: reduce1(1)), (6, lambda: reduce1(0)), (10, lambda: reduce2(1)), (12, lambda: reduce3(1))):
+            for at, act in ((2, lambda: reduce1(1)), (6, lambda: reduce1(0)), (10, lambda: reduce2(1))):
                 @pl.when(jnp.logical_and(sweep == 1, o == at))
                 def _(act=act):
                     act()
 
             kc = order(o)
             for blk in range(2):
-                chunk(grads, blk, kc, [8 * blk + 4 * layer + n for n in range(4)])
+                chunk(grads, blk, kc, [2 * blk + layer])
             return carry
 
         lax.fori_loop(0, 16, cell, 0)
+
+        @pl.when(sweep == 1)
+        def _():
+            reduce2(0)
+
         finish(layer)
 
         @pl.when(sweep == 0)
@@ -450,7 +441,7 @@
     lax.fori_loop(0, 2, rows, 0)
     back[1].start()
     mine.start()
-    reduce2(0)
+    reduce3(1)
     reduce4(1)
     reduce3(0)
     reduce5(1)
@@ -465,7 +456,7 @@
     mine.wait()
     for copy in back:
         copy.wait()
-    for copy in sum(ex[0] + ex[1] + ex[2], []) + near0 + onward0 + near1 + onward1 + first + second + third + fourth:
+    for copy in sum(ex[0] + ex[1] + ex[2], []) + y_copies[1:] + sum(z_sent, []) + first + second + third + fourth:
         copy.wait_send()
     for t in range(2):
         to_self, pairs = a_copies(t)
@@ -522,7 +513,8 @@
             pltpu.VMEM((2, 2, 128, 128), f32),
             dma((2, 3, 2)), dma((2, 3, 2)), dma((3,)),
             dma((2, 2)), dma((2, 2)),
-            dma((2, 2, 4)), dma((2, 2, 4)),
+            pltpu.SemaphoreType.REGULAR,
+            dma((3,)), dma((3,)), dma((4, 3)), dma((4, 3)),
             dma((4, 2, 2)), dma((4, 2, 2)),
             dma((2,)), dma((2,)),
             dma((3,)), dma((3,)),

time: 150 us -> 113 us (0.75)
  the two profiles are of different devices: /device:TPU:104 before, /device:TPU:1 now
where the time goes in v3:
time: 113 us; the launch traced here: 111 us
  Pallas kernels  107 us (95%)
  local copies, waits for them, and re-layouts  3.68 us (3%)
    pallas_call x1, Pallas kernels, body(): pl.pallas_call(kernel, out_shape=(jax.ShapeDtypeStruct((128, 4096), bf16)...  107 us
    unnamed x7, local copies, waits for them, and re-layouts  3.68 us

profile of v3, /device:TPU:1, one launch (start us, length us, event | category | flops | bytes accessed | tf_op | source)
XLA Modules:
  0.0 111.2 jit_solution(3357179671195592416)
XLA Ops:
  0.6 106.8 %shard_map.67 = (bf16[128,4096]{1,0:T(8,128)(2,1)}, bf16[128,128]{1,0:T(8,128)(2,1)}, bf16[128,128]{1,0:T(8,128)(2,1)}) custom-call(bf16[128,4096]{1,0:T(8,128)(2,1)} %bitcast.4, bf16[128,128]{1,0:T(8,128)(2,1)} %k_in.1, bf16[128,128]{1,0:T(8,128)(2,1)} %v_in.1, bf16[128,4096]{1,0:T(8,128)(2,1)} %bitcast.5), custom_call_target="tpu_custom_call" | custom-call | flops 16000000000 | bytes 4194304 | tf_op jit(solution)/shard_map/pallas_call | solution.py:479
  107.5 0.0 copy-start.1
  107.5 2.3 %copy.10 = bf16[1,128,4096]{2,1,0:T(8,128)(2,1)} copy(bf16[1,128,4096]{2,1,0:T(8,128)(2,1)} %bitcast.3) | data formatting | bytes 2097152
  109.8 0.0 copy-done.1
  109.8 0.0 copy-start
  109.8 0.6 copy.11
  110.4 0.2 copy-done
  110.5 0.6 copy.12
Async XLA Ops:
  107.5 2.3 %copy-start.1 = (bf16[128,128]{1,0:T(8,128)(2,1)S(1)}, bf16[128,128]{1,0:T(8,128)(2,1)}, u32[]{:S(2)}) copy-start(bf16[128,128]{1,0:T(8,128)(2,1)} %get-tuple-element.13) | copy-start | bytes 98308
  109.8 0.8 copy-start

commit v4 on v3

--- a/solution.py
+++ b/solution.py
@@ -30,9 +30,9 @@
     dq_out, dk_out, dv_out,
     q_s, g_s, dq_s, kv, q_t, g_t, k_t, acc, dkv,
     m8, l8, d8, top, rdot,
-    st1, rc1, st2, rc2, red, st3, rc3, st4, rc4, fin, rcx,
+    zst, zrc, fst, frc, cst, crc, fin, rcx,
     ex_send, ex_recv, loc, a_send, a_recv, clear_sem, y_send, y_recv, z_send, z_recv,
-    rs_send, rs_recv, x_send, x_recv, dq_send, dq_recv,
+    zr_send, zr_recv, f_send, f_recv, c_send, c_recv, x_send, x_recv, dq_send, dq_recv,
 ):
     pipe = lax.axis_index("pipe")
     seq = lax.axis_index("seq")
@@ -305,158 +305,107 @@
     top[...] = high * EXPO + jnp.log2(total)
     rdot[...] = jnp.sum(d8[...] * fold, axis=0, keepdims=True) / total
 
-    def part_of(h, i, d):
-        return dkv[i, 0, :, d] if h == 0 else dkv[i, 1, d, :]
-
-    spots = (z, y)
-    rings = ((z_up, z_dn), (y_up, y_dn))
-    first, second, third, fourth = [], [], [], []
-    for h in range(2):
-        up, dn = rings[h]
-        first.append(remote(st1.at[h, 0], rc1.at[h, 0], rs_send.at[0, h, 0], rs_recv.at[0, h, 0], dn))
-        first.append(remote(st1.at[h, 1], rc1.at[h, 1], rs_send.at[0, h, 1], rs_recv.at[0, h, 1], up))
-        second.append(remote(st2.at[h, 0], rc2.at[h, 0], rs_send.at[1, h, 0], rs_recv.at[1, h, 0], dn))
-        second.append(remote(st2.at[h, 1], rc2.at[h, 1], rs_send.at[1, h, 1], rs_recv.at[1, h, 1], up))
-        up, dn = rings[1 - h]
-        third.append(remote(st3.at[h, 0], rc3.at[h, 0], rs_send.at[2, h, 0], rs_recv.at[2, h, 0], dn))
-        third.append(remote(st3.at[h, 1], rc3.at[h, 1], rs_send.at[2, h, 1], rs_recv.at[2, h, 1], up))
-        fourth.append(remote(st4.at[h, 0], rc4.at[h, 0], rs_send.at[3, h, 0], rs_recv.at[3, h, 0], dn))
-        fourth.append(remote(st4.at[h, 1], rc4.at[h, 1], rs_send.at[3, h, 1], rs_recv.at[3, h, 1], up))
-
-    def reduce1(h):
-        far = (spots[h] + 2) % 4
-        st1[h, 0] = part_of(h, 0, far).astype(bf16)
-        first[2 * h].start()
-        st1[h, 1] = part_of(h, 1, far).astype(bf16)
-        first[2 * h + 1].start()
-
-    def reduce2(h):
-        spot = spots[h]
-        st2[h, 0, 1] = part_of(h, 1, (spot + 3) % 4).astype(bf16)
-        st2[h, 1, 0] = part_of(h, 0, (spot + 1) % 4).astype(bf16)
-        first[2 * h].wait_recv()
-        st2[h, 0, 0] = (part_of(h, 0, (spot + 3) % 4) + rc1[h, 0].astype(f32)).astype(bf16)
-        second[2 * h].start()
-        first[2 * h + 1].wait_recv()
-        st2[h, 1, 1] = (part_of(h, 1, (spot + 1) % 4) + rc1[h, 1].astype(f32)).astype(bf16)
-        second[2 * h + 1].start()
-
-    def reduce3(h):
-        second[2 * h].wait_recv()
-        second[2 * h + 1].wait_recv()
-        for i in range(2):
-            red[h, i] = part_of(h, i, spots[h]) + rc2[h, 0, i].astype(f32) + rc2[h, 1, i].astype(f32)
-        spot = spots[1 - h]
-        far = (spot + 2) % 4
-        st3[h, 0] = red[h, 0, far]
-        third[2 * h].start()
-        st3[h, 1] = red[h, 1, far]
-        third[2 * h + 1].start()
-        st4[h, 0, 1] = red[h, 1, (spot + 3) % 4]
-        st4[h, 1, 0] = red[h, 0, (spot + 1) % 4]
-
-    def reduce4(h):
-        spot = spots[1 - h]
-        third[2 * h].wait_recv()
-        st4[h, 0, 0] = red[h, 0, (spot + 3) % 4] + rc3[h, 0]
-        fourth[2 * h].start()
-        third[2 * h + 1].wait_recv()
-        st4[h, 1, 1] = red[h, 1, (spot + 1) % 4] + rc3[h, 1]
-        fourth[2 * h + 1].start()
+    def term(g, d):
+        return dkv.at[:, :, y_of(g), (z + d) % 4]
+
+    zr_copies = [
+        [remote(zst.at[g, d], zrc.at[g, d], zr_send.at[g, d], zr_recv.at[g, d], z_all[d]) for d in range(3)] for g in range(4)
+    ]
+    f_copies = [remote(fst.at[n], frc.at[n], f_send.at[n], f_recv.at[n], y_all[1]) for n in range(2)]
+    c_copy = remote(cst, crc, c_send, c_recv, y_all[0])
+
+    def along_z(g):
+        for d, step in enumerate((1, 3, 2)):
+            zst[g, d] = term(g, step)[...].astype(bf16)
+            zr_copies[g][d].start()
+
+    def summed(g):
+        for d in range(3):
+            zr_copies[g][d].wait_recv()
+        return term(g, 0)[...] + zrc[g, 0].astype(f32) + zrc[g, 1].astype(f32) + zrc[g, 2].astype(f32)
+
+    def over_free(n):
+        fst[n] = summed(3 - n).astype(bf16)
+        f_copies[n].start()
+
+    def over_cross():
+        part = summed(1)
+        f_copies[0].wait_recv()
+        cst[...] = (part + frc[0].astype(f32)).astype(bf16)
+        c_copy.start()
 
     def x_copies(h):
         to_self = jnp.logical_and(x_hi == x_lo, h == x_lo)
-        local = pltpu.make_async_copy(fin.at[h], rcx.at[x_hi], x_recv.at[x_hi])
-        away = remote(fin.at[h], rcx.at[x_hi], x_send.at[h], x_recv.at[x_hi], x_from(h))
+        local = pltpu.make_async_copy(fin.at[:, h], rcx.at[x_hi], x_recv.at[x_hi])
+        away = remote(fin.at[:, h], rcx.at[x_hi], x_send.at[h], x_recv.at[x_hi], x_from(h))
         return to_self, local, away
 
-    def reduce5(h):
-        fourth[2 * h].wait_recv()
-        fourth[2 * h + 1].wait_recv()
-        for i in range(2):
-            fin[h, i] = red[h, i, spots[1 - h]] + rc4[h, 0, i] + rc4[h, 1, i]
-        to_self, local, away = x_copies(h)
-
-        @pl.when(to_self)
-        def _():
-            local.start()
-
-        @pl.when(jnp.logical_not(to_self))
-        def _():
-            away.start()
-
-    def finish(layer):
+    def along_x():
+        part = summed(0)
+        f_copies[1].wait_recv()
+        c_copy.wait_recv()
+        fin[...] = part + frc[1].astype(f32) + crc[...].astype(f32)
+        for h in range(2):
+            to_self, local, away = x_copies(h)
+
+            @pl.when(to_self)
+            def _(local=local):
+                local.start()
+
+            @pl.when(jnp.logical_not(to_self))
+            def _(away=away):
+                away.start()
+
+    events = (
+        (4, lambda: along_z(3)), (8, lambda: along_z(2)), (10, lambda: over_free(0)),
+        (12, lambda: along_z(1)), (14, lambda: over_free(1)),
+    )
+
+    def second_rows(o, carry):
+        for at, act in events:
+            @pl.when(o == at)
+            def _(act=act):
+                act()
+
+        kc = ((o // 2) % 2) * 8 + y_of(3 - o // 4) * 2 + o % 2
         for blk in range(2):
-            s = 2 * blk + layer
-            for n in range(4):
-                t = (acc[:, lanes((s * 4 + n) * 256, 256)] * SCALE).T.astype(bf16)
-                dq_s[s, :, lanes(n * 256, 128)] = t[:128]
-                dq_s[s, :, lanes(n * 256 + 128, 128)] = t[128:]
-
-    mine = pltpu.make_async_copy(dq_s.at[core], dq_out.at[:, own_cols], loc.at[2])
+            chunk(grads, blk, kc, [2 * blk, 2 * blk + 1])
+        return carry
+
+    lax.fori_loop(0, 16, second_rows, 0)
+    along_z(0)
+    over_cross()
+
+    def finish(s):
+        for n in range(4):
+            t = (acc[:, lanes((s * 4 + n) * 256, 256)] * SCALE).T.astype(bf16)
+            dq_s[s, :, lanes(n * 256, 128)] = t[:128]
+            dq_s[s, :, lanes(n * 256 + 128, 128)] = t[128:]
+
     back = [
         remote(dq_s.at[2 * flip + c_t], dq_out.at[:, own_cols], dq_send.at[n], dq_recv.at[n], mates[n])
         for n, (c_t, flip) in enumerate(((1 - core, 0), (core, 1), (1 - core, 1)))
     ]
-
-    def rows(sweep, carry):
-        layer = (core + 1 + sweep) % 2
-
-        def cell(o, carry):
-            for at, act in ((2, lambda: reduce1(1)), (6, lambda: reduce1(0)), (10, lambda: reduce2(1))):
-                @pl.when(jnp.logical_and(sweep == 1, o == at))
-                def _(act=act):
-                    act()
-
-            kc = order(o)
-            for blk in range(2):
-                chunk(grads, blk, kc, [2 * blk + layer])
-            return carry
-
-        lax.fori_loop(0, 16, cell, 0)
-
-        @pl.when(sweep == 1)
-        def _():
-            reduce2(0)
-
-        finish(layer)
-
-        @pl.when(sweep == 0)
-        def _():
-            back[0].start()
-            back[2].start()
-
-        return carry
-
-    def order(o):
-        pick = [
-            8 + ((y + 2) % 4) * 2 + o,
-            (o - 2) * 2 + 1 - z // 2,
-            8 + ((y + 1 + 2 * ((o - 6) // 2) - (o - 6) // 4) % 4) * 2 + o % 2,
-            (o - 12) * 2 + z // 2,
-        ]
-        g1, g2, g3 = (o + 14) // 16, (o + 10) // 16, (o + 4) // 16
-        return pick[0] * (1 - g1) + pick[1] * (g1 - g2) + pick[2] * (g2 - g3) + pick[3] * g3
-
-    lax.fori_loop(0, 2, rows, 0)
+    mine = pltpu.make_async_copy(dq_s.at[core], dq_out.at[:, own_cols], loc.at[2])
+    finish(2 + core)
     back[1].start()
+    finish(3 - core)
+    back[2].start()
+    finish(1 - core)
+    back[0].start()
+    finish(core)
     mine.start()
-    reduce3(1)
-    reduce4(1)
-    reduce3(0)
-    reduce5(1)
-    reduce4(0)
-    reduce5(0)
+    along_x()
 
     for s in range(2):
-        pltpu.make_async_copy(fin.at[0], rcx.at[s], x_recv.at[s]).wait()
+        pltpu.make_async_copy(fin.at[:, 0], rcx.at[s], x_recv.at[s]).wait()
     dk_out[...] = ((rcx[0, 0] + rcx[1, 0]) * SCALE).astype(bf16)
     dv_out[...] = (rcx[0, 1] + rcx[1, 1]).astype(bf16)
 
     mine.wait()
     for copy in back:
         copy.wait()
-    for copy in sum(ex[0] + ex[1] + ex[2], []) + y_copies[1:] + sum(z_sent, []) + first + second + third + fourth:
+    for copy in sum(ex[0] + ex[1] + ex[2], []) + y_copies[1:] + sum(z_sent, []) + sum(zr_copies, []) + f_copies + [c_copy]:
         copy.wait_send()
     for t in range(2):
         to_self, pairs = a_copies(t)
@@ -475,7 +424,7 @@
 def body(queries, shared_keys, shared_values, out_grad):
     any_, vmem = pl.BlockSpec(memory_space=pl.ANY), pl.BlockSpec(memory_space=pltpu.VMEM)
     dma = pltpu.SemaphoreType.DMA
-    big, small = (2, 2, 4, 128, 128), (2, 2, 2, 128, 128)
+    part = (2, 2, 128, 128)
     dq, dk, dv = pl.pallas_call(
         kernel,
         out_shape=(
@@ -500,22 +449,19 @@
             pltpu.VMEM((8, 4096), f32),
             pltpu.VMEM((1, 4096), f32),
             pltpu.VMEM((1, 4096), f32),
-            pltpu.VMEM(big, bf16),
-            pltpu.VMEM(big, bf16),
-            pltpu.VMEM((2,) + big, bf16),
-            pltpu.VMEM((2,) + big, bf16),
-            pltpu.VMEM(big, f32),
-            pltpu.VMEM((2, 2, 128, 128), f32),
-            pltpu.VMEM((2, 2, 128, 128), f32),
-            pltpu.VMEM(small, f32),
-            pltpu.VMEM(small, f32),
-            pltpu.VMEM((2, 2, 128, 128), f32),
-            pltpu.VMEM((2, 2, 128, 128), f32),
+            pltpu.VMEM((4, 3) + part, bf16),
+            pltpu.VMEM((4, 3) + part, bf16),
+            pltpu.VMEM((2,) + part, bf16),
+            pltpu.VMEM((2,) + part, bf16),
+            pltpu.VMEM(part, bf16),
+            pltpu.VMEM(part, bf16),
+            pltpu.VMEM(part, f32),
+            pltpu.VMEM(part, f32),
             dma((2, 3, 2)), dma((2, 3, 2)), dma((3,)),
             dma((2, 2)), dma((2, 2)),
             pltpu.SemaphoreType.REGULAR,
             dma((3,)), dma((3,)), dma((4, 3)), dma((4, 3)),
-            dma((4, 2, 2)), dma((4, 2, 2)),
+            dma((4, 3)), dma((4, 3)), dma((2,)), dma((2,)), dma, dma,
             dma((2,)), dma((2,)),
             dma((3,)), dma((3,)),
         ],

time: 113 us -> 107 us (0.947)
  Pallas kernels: 107 us -> 102 us
    pallas_call x1, Pallas kernels: 107 us -> 102 us  [body(): pl.pallas_call(kernel, out_shape=(jax.ShapeDtypeStruct((128, 4096), bf16)...]
where the time goes in v4:
time: 107 us; the launch traced here: 106 us
  Pallas kernels  102 us (95%)
  local copies, waits for them, and re-layouts  3.68 us (3%)
    pallas_call x1, Pallas kernels, body(): pl.pallas_call(kernel, out_shape=(jax.ShapeDtypeStruct((128, 4096), bf16)...  102 us
    unnamed x7, local copies, waits for them, and re-layouts  3.68 us

profile of v4, /device:TPU:1, one launch (start us, length us, event | category | flops | bytes accessed | tf_op | source)
XLA Modules:
  0.0 106.2 jit_solution(9241240444872950369)
XLA Ops:
  0.6 101.9 %shard_map.67 = (bf16[128,4096]{1,0:T(8,128)(2,1)}, bf16[128,128]{1,0:T(8,128)(2,1)}, bf16[128,128]{1,0:T(8,128)(2,1)}) custom-call(bf16[128,4096]{1,0:T(8,128)(2,1)} %bitcast.4, bf16[128,128]{1,0:T(8,128)(2,1)} %k_in.1, bf16[128,128]{1,0:T(8,128)(2,1)} %v_in.1, bf16[128,4096]{1,0:T(8,128)(2,1)} %bitcast.5), custom_call_target="tpu_custom_call" | custom-call | flops 16000000000 | bytes 4194304 | tf_op jit(solution)/shard_map/pallas_call | solution.py:428
  102.5 0.0 copy-start.1
  102.5 2.3 %copy.10 = bf16[1,128,4096]{2,1,0:T(8,128)(2,1)} copy(bf16[1,128,4096]{2,1,0:T(8,128)(2,1)} %bitcast.3) | data formatting | bytes 2097152
  104.8 0.0 copy-done.1
  104.8 0.0 copy-start
  104.8 0.6 copy.11
  105.5 0.2 copy-done
  105.6 0.6 copy.12
Async XLA Ops:
  102.5 2.3 %copy-start.1 = (bf16[128,128]{1,0:T(8,128)(2,1)S(1)}, bf16[128,128]{1,0:T(8,128)(2,1)}, u32[]{:S(2)}) copy-start(bf16[128,128]{1,0:T(8,128)(2,1)} %get-tuple-element.13) | copy-start | bytes 98308
  104.8 0.8 copy-start

commit v5 on v4

--- a/solution.py
+++ b/solution.py
@@ -32,7 +32,7 @@
     m8, l8, d8, top, rdot,
     zst, zrc, fst, frc, cst, crc, fin, rcx,
     ex_send, ex_recv, loc, a_send, a_recv, clear_sem, y_send, y_recv, z_send, z_recv,
-    zr_send, zr_recv, f_send, f_recv, c_send, c_recv, x_send, x_recv, dq_send, dq_recv,
+    zr_send, zr_recv, zl_send, zl_recv, f_send, f_recv, c_send, c_recv, x_send, x_recv, dq_send, dq_recv,
 ):
     pipe = lax.axis_index("pipe")
     seq = lax.axis_index("seq")
@@ -305,24 +305,40 @@
     top[...] = high * EXPO + jnp.log2(total)
     rdot[...] = jnp.sum(d8[...] * fold, axis=0, keepdims=True) / total
 
-    def term(g, d):
-        return dkv.at[:, :, y_of(g), (z + d) % 4]
+    z_spot = (z + 1 - 2 * (z % 2), (z + 2) % 4, 3 - z)
+    z_peer = [dev(x_hi, core, x_lo, y, spot) for spot in z_spot]
+
+    def term(g, spot):
+        return dkv.at[:, :, y_of(g), spot]
 
     zr_copies = [
-        [remote(zst.at[g, d], zrc.at[g, d], zr_send.at[g, d], zr_recv.at[g, d], z_all[d]) for d in range(3)] for g in range(4)
+        [remote(zst.at[g, d], zrc.at[g, d], zr_send.at[g, d], zr_recv.at[g, d], z_peer[d]) for d in range(3)]
+        for g in range(1, 4)
+    ]
+    last_copies = [
+        [
+            remote(zst.at[0, d, :, h], zrc.at[0, d, :, h], zl_send.at[h, d], zl_recv.at[h, d], z_peer[d])
+            for d in range(3)
+        ]
+        for h in range(2)
     ]
     f_copies = [remote(fst.at[n], frc.at[n], f_send.at[n], f_recv.at[n], y_all[1]) for n in range(2)]
     c_copy = remote(cst, crc, c_send, c_recv, y_all[0])
 
     def along_z(g):
-        for d, step in enumerate((1, 3, 2)):
-            zst[g, d] = term(g, step)[...].astype(bf16)
-            zr_copies[g][d].start()
+        for d in range(3):
+            zst[g, d] = term(g, z_spot[d])[...].astype(bf16)
+            zr_copies[g - 1][d].start()
+
+    def last_along_z(h, parts):
+        for d in parts:
+            zst[0, d, :, h] = dkv[:, h, y, z_spot[d]].astype(bf16)
+            last_copies[h][d].start()
 
     def summed(g):
-        for d in range(3):
-            zr_copies[g][d].wait_recv()
-        return term(g, 0)[...] + zrc[g, 0].astype(f32) + zrc[g, 1].astype(f32) + zrc[g, 2].astype(f32)
+        for copy in zr_copies[g - 1] if g else last_copies[0] + last_copies[1]:
+            copy.wait_recv()
+        return term(g, z)[...] + zrc[g, 0].astype(f32) + zrc[g, 1].astype(f32) + zrc[g, 2].astype(f32)
 
     def over_free(n):
         fst[n] = summed(3 - n).astype(bf16)
@@ -356,26 +372,6 @@
             def _(away=away):
                 away.start()
 
-    events = (
-        (4, lambda: along_z(3)), (8, lambda: along_z(2)), (10, lambda: over_free(0)),
-        (12, lambda: along_z(1)), (14, lambda: over_free(1)),
-    )
-
-    def second_rows(o, carry):
-        for at, act in events:
-            @pl.when(o == at)
-            def _(act=act):
-                act()
-
-        kc = ((o // 2) % 2) * 8 + y_of(3 - o // 4) * 2 + o % 2
-        for blk in range(2):
-            chunk(grads, blk, kc, [2 * blk, 2 * blk + 1])
-        return carry
-
-    lax.fori_loop(0, 16, second_rows, 0)
-    along_z(0)
-    over_cross()
-
     def finish(s):
         for n in range(4):
             t = (acc[:, lanes((s * 4 + n) * 256, 256)] * SCALE).T.astype(bf16)
@@ -387,12 +383,45 @@
         for n, (c_t, flip) in enumerate(((1 - core, 0), (core, 1), (1 - core, 1)))
     ]
     mine = pltpu.make_async_copy(dq_s.at[core], dq_out.at[:, own_cols], loc.at[2])
+    def when(cond, *acts):
+        @pl.when(cond)
+        def _():
+            for act in acts:
+                act()
+
+    def chunk_at(g, o):
+        return (o // 2) * 8 + y_of(g) * 2 + (z // 2 + 1 + o) % 2
+
+    def second_rows(o, carry):
+        when(o == 4, lambda: along_z(3))
+        when(o == 8, lambda: along_z(2))
+        when(o == 10, lambda: over_free(0))
+        for blk in range(2):
+            chunk(grads, blk, chunk_at(3 - o // 4, o % 4), [2 * blk, 2 * blk + 1])
+        return carry
+
+    lax.fori_loop(0, 12, second_rows, 0)
+    along_z(1)
+
+    def third_rows(o, carry):
+        when(o == 2, lambda: over_free(1))
+        when(
+            o == 4,
+            lambda: finish(3 - core), lambda: back[2].start(),
+            lambda: finish(1 - core), lambda: back[0].start(),
+        )
+        layer = (core + 1 + o // 4) % 2
+        for blk in range(2):
+            chunk(grads, blk, chunk_at(0, o % 4), [2 * blk + layer])
+        for h in range(2):
+            when(o == 4 + 2 * h, lambda: last_along_z(h, (1, 2)))
+            when(o == 5 + 2 * h, lambda: last_along_z(h, (0,)))
+        return carry
+
+    lax.fori_loop(0, 8, third_rows, 0)
+    over_cross()
     finish(2 + core)
     back[1].start()
-    finish(3 - core)
-    back[2].start()
-    finish(1 - core)
-    back[0].start()
     finish(core)
     mine.start()
     along_x()
@@ -405,7 +434,7 @@
     mine.wait()
     for copy in back:
         copy.wait()
-    for copy in sum(ex[0] + ex[1] + ex[2], []) + y_copies[1:] + sum(z_sent, []) + sum(zr_copies, []) + f_copies + [c_copy]:
+    for copy in sum(ex[0] + ex[1] + ex[2], []) + y_copies[1:] + sum(z_sent, []) + sum(zr_copies + last_copies, []) + f_copies + [c_copy]:
         copy.wait_send()
     for t in range(2):
         to_self, pairs = a_copies(t)
@@ -461,7 +490,7 @@
             dma((2, 2)), dma((2, 2)),
             pltpu.SemaphoreType.REGULAR,
             dma((3,)), dma((3,)), dma((4, 3)), dma((4, 3)),
-            dma((4, 3)), dma((4, 3)), dma((2,)), dma((2,)), dma, dma,
+            dma((4, 3)), dma((4, 3)), dma((2, 3)), dma((2, 3)), dma((2,)), dma((2,)), dma, dma,
             dma((2,)), dma((2,)),
             dma((3,)), dma((3,)),
         ],

time: 107 us -> 102 us (0.953)
  Pallas kernels: 102 us -> 96.7 us
    pallas_call x1, Pallas kernels: 102 us -> 96.7 us  [body(): pl.pallas_call(kernel, out_shape=(jax.ShapeDtypeStruct((128, 4096), bf16)...]
where the time goes in v5:
time: 102 us; the launch traced here: 101 us
  Pallas kernels  96.7 us (95%)
  local copies, waits for them, and re-layouts  3.68 us (4%)
    pallas_call x1, Pallas kernels, body(): pl.pallas_call(kernel, out_shape=(jax.ShapeDtypeStruct((128, 4096), bf16)...  96.7 us
    unnamed x7, local copies, waits for them, and re-layouts  3.68 us

profile of v5, /device:TPU:1, one launch (start us, length us, event | category | flops | bytes accessed | tf_op | source)
XLA Modules:
  0.0 101.1 jit_solution(761891886472289766)
XLA Ops:
  0.6 96.7 %shard_map.67 = (bf16[128,4096]{1,0:T(8,128)(2,1)}, bf16[128,128]{1,0:T(8,128)(2,1)}, bf16[128,128]{1,0:T(8,128)(2,1)}) custom-call(bf16[128,4096]{1,0:T(8,128)(2,1)} %bitcast.4, bf16[128,128]{1,0:T(8,128)(2,1)} %k_in.1, bf16[128,128]{1,0:T(8,128)(2,1)} %v_in.1, bf16[128,4096]{1,0:T(8,128)(2,1)} %bitcast.5), custom_call_target="tpu_custom_call" | custom-call | flops 16000000000 | bytes 4194304 | tf_op jit(solution)/shard_map/pallas_call | solution.py:457
  97.4 0.0 copy-start.1
  97.4 2.3 %copy.10 = bf16[1,128,4096]{2,1,0:T(8,128)(2,1)} copy(bf16[1,128,4096]{2,1,0:T(8,128)(2,1)} %bitcast.3) | data formatting | bytes 2097152
  99.7 0.0 copy-done.1
  99.7 0.0 copy-start
  99.7 0.6 copy.11
  100.3 0.2 copy-done
  100.5 0.6 copy.12
Async XLA Ops:
  97.4 2.3 %copy-start.1 = (bf16[128,128]{1,0:T(8,128)(2,1)S(1)}, bf16[128,128]{1,0:T(8,128)(2,1)}, u32[]{:S(2)}) copy-start(bf16[128,128]{1,0:T(8,128)(2,1)} %get-tuple-element.13) | copy-start | bytes 98308
  99.7 0.8 copy-start

commit v6 on v5

--- a/solution.py
+++ b/solution.py
@@ -32,7 +32,7 @@
     m8, l8, d8, top, rdot,
     zst, zrc, fst, frc, cst, crc, fin, rcx,
     ex_send, ex_recv, loc, a_send, a_recv, clear_sem, y_send, y_recv, z_send, z_recv,
-    zr_send, zr_recv, zl_send, zl_recv, f_send, f_recv, c_send, c_recv, x_send, x_recv, dq_send, dq_recv,
+    zr_send, zr_recv, f_send, f_recv, c_send, c_recv, x_send, x_recv, dq_send, dq_recv,
 ):
     pipe = lax.axis_index("pipe")
     seq = lax.axis_index("seq")
@@ -143,20 +143,24 @@
             def _(away=away):
                 away.start()
 
-    def exchange(n, half):
+    def exchange(n, piece):
+        start, width = ((0, 256), (256, 256), (512, 512))[piece]
         c_t, flip = ((1 - core, 0), (core, 1), (1 - core, 1))[n]
         x_t = (1 - x_lo) if flip else x_lo
-        cols = lanes((2 * x_t + c_t) * 1024 + half * 512, 512)
-        there = lanes(half * 512, 512)
+        cols = lanes((2 * x_t + c_t) * 1024 + start, width)
+        there = lanes(start, width)
         slot = 2 * flip + core
         return [
-            remote(src.at[:, cols], dst.at[slot, :, there], ex_send.at[i, n, half], ex_recv.at[i, n, half], mates[n])
+            remote(src.at[:, cols], dst.at[slot, :, there], ex_send.at[i, n, piece], ex_recv.at[i, n, piece], mates[n])
             for i, (src, dst) in enumerate(((q_in, q_s), (g_in, g_s)))
         ]
 
-    ex = [[exchange(n, half) for half in range(2)] for n in range(3)]
-    for half in range(2):
-        for copy in ex[0][half]:
+    ex = [[exchange(n, piece) for piece in range(3)] for n in range(3)]
+    for n in (1, 2):
+        for copy in ex[n][0]:
+            copy.start()
+    for piece in range(3):
+        for copy in ex[0][piece]:
             copy.start()
 
     for i in range(2):
@@ -187,15 +191,15 @@
     for copy in z_sent[2]:
         copy.start()
     pl.semaphore_wait(clear_sem, 3)
-    for half in range(2):
+    for piece in (1, 2):
         for n in (1, 2):
-            for copy in ex[n][half]:
+            for copy in ex[n][piece]:
                 copy.start()
     y_copies[2].wait_recv()
     for copy in z_sent[3]:
         copy.start()
-    for half in range(2):
-        for copy in ex[0][half]:
+    for piece in range(3):
+        for copy in ex[0][piece]:
             copy.wait_recv()
     lax.fori_loop(0, 4, lambda n, carry: prep((1 - core) * 4 + n), 0)
 
@@ -264,7 +268,7 @@
 
     def far_arrive(half):
         for n in (1, 2):
-            for copy in ex[n][half]:
+            for copy in ex[n][2] if half else ex[n][0] + ex[n][1]:
                 copy.wait_recv()
         for i in far_tiles(half):
             prep(i)
@@ -311,32 +315,20 @@
     def term(g, spot):
         return dkv.at[:, :, y_of(g), spot]
 
-    zr_copies = [
-        [remote(zst.at[g, d], zrc.at[g, d], zr_send.at[g, d], zr_recv.at[g, d], z_peer[d]) for d in range(3)]
-        for g in range(1, 4)
-    ]
-    last_copies = [
-        [
-            remote(zst.at[0, d, :, h], zrc.at[0, d, :, h], zl_send.at[h, d], zl_recv.at[h, d], z_peer[d])
-            for d in range(3)
-        ]
-        for h in range(2)
-    ]
+    def z_copy(g, h, d):
+        return remote(zst.at[g, d, :, h], zrc.at[g, d, :, h], zr_send.at[g, h, d], zr_recv.at[g, h, d], z_peer[d])
+
+    zr_copies = [[z_copy(g, h, d) for h in range(2) for d in range(3)] for g in range(4)]
     f_copies = [remote(fst.at[n], frc.at[n], f_send.at[n], f_recv.at[n], y_all[1]) for n in range(2)]
     c_copy = remote(cst, crc, c_send, c_recv, y_all[0])
 
-    def along_z(g):
-        for d in range(3):
-            zst[g, d] = term(g, z_spot[d])[...].astype(bf16)
-            zr_copies[g - 1][d].start()
-
-    def last_along_z(h, parts):
+    def along_z(g, h, parts):
         for d in parts:
-            zst[0, d, :, h] = dkv[:, h, y, z_spot[d]].astype(bf16)
-            last_copies[h][d].start()
+            zst[g, d, :, h] = dkv[:, h, y_of(g), z_spot[d]].astype(bf16)
+            z_copy(g, h, d).start()
 
     def summed(g):
-        for copy in zr_copies[g - 1] if g else last_copies[0] + last_copies[1]:
+        for copy in zr_copies[g]:
             copy.wait_recv()
         return term(g, z)[...] + zrc[g, 0].astype(f32) + zrc[g, 1].astype(f32) + zrc[g, 2].astype(f32)
 
@@ -360,7 +352,7 @@
         part = summed(0)
         f_copies[1].wait_recv()
         c_copy.wait_recv()
-        fin[...] = part + frc[1].astype(f32) + crc[...].astype(f32)
+        fin[...] = (part + frc[1].astype(f32) + crc[...].astype(f32)).astype(bf16)
         for h in range(2):
             to_self, local, away = x_copies(h)
 
@@ -392,34 +384,34 @@
     def chunk_at(g, o):
         return (o // 2) * 8 + y_of(g) * 2 + (z // 2 + 1 + o) % 2
 
+    def send_parts(g, o):
+        for h in range(2):
+            when(o == 2 * h, lambda: along_z(g, h, (1, 2)))
+            when(o == 2 * h + 1, lambda: along_z(g, h, (0,)))
+
     def second_rows(o, carry):
-        when(o == 4, lambda: along_z(3))
-        when(o == 8, lambda: along_z(2))
-        when(o == 10, lambda: over_free(0))
+        when(o == 8, lambda: over_free(0))
         for blk in range(2):
             chunk(grads, blk, chunk_at(3 - o // 4, o % 4), [2 * blk, 2 * blk + 1])
+        send_parts(3 - o // 4, o % 4)
         return carry
 
     lax.fori_loop(0, 12, second_rows, 0)
-    along_z(1)
 
     def third_rows(o, carry):
-        when(o == 2, lambda: over_free(1))
+        when(o == 0, lambda: over_free(1))
         when(
-            o == 4,
+            o == 4, over_cross,
             lambda: finish(3 - core), lambda: back[2].start(),
             lambda: finish(1 - core), lambda: back[0].start(),
         )
         layer = (core + 1 + o // 4) % 2
         for blk in range(2):
             chunk(grads, blk, chunk_at(0, o % 4), [2 * blk + layer])
-        for h in range(2):
-            when(o == 4 + 2 * h, lambda: last_along_z(h, (1, 2)))
-            when(o == 5 + 2 * h, lambda: last_along_z(h, (0,)))
+        send_parts(0, o - 4)
         return carry
 
     lax.fori_loop(0, 8, third_rows, 0)
-    over_cross()
     finish(2 + core)
     back[1].start()
     finish(core)
@@ -428,13 +420,14 @@
 
     for s in range(2):
         pltpu.make_async_copy(fin.at[:, 0], rcx.at[s], x_recv.at[s]).wait()
-    dk_out[...] = ((rcx[0, 0] + rcx[1, 0]) * SCALE).astype(bf16)
-    dv_out[...] = (rcx[0, 1] + rcx[1, 1]).astype(bf16)
+    total = rcx[0].astype(f32) + rcx[1].astype(f32)
+    dk_out[...] = (total[0] * SCALE).astype(bf16)
+    dv_out[...] = total[1].astype(bf16)
 
     mine.wait()
     for copy in back:
         copy.wait()
-    for copy in sum(ex[0] + ex[1] + ex[2], []) + y_copies[1:] + sum(z_sent, []) + sum(zr_copies + last_copies, []) + f_copies + [c_copy]:
+    for copy in sum(ex[0] + ex[1] + ex[2], []) + y_copies[1:] + sum(z_sent, []) + sum(zr_copies, []) + f_copies + [c_copy]:
         copy.wait_send()
     for t in range(2):
         to_self, pairs = a_copies(t)
@@ -484,13 +477,13 @@
             pltpu.VMEM((2,) + part, bf16),
             pltpu.VMEM(part, bf16),
             pltpu.VMEM(part, bf16),
-            pltpu.VMEM(part, f32),
-            pltpu.VMEM(part, f32),
-            dma((2, 3, 2)), dma((2, 3, 2)), dma((3,)),
+            pltpu.VMEM(part, bf16),
+            pltpu.VMEM(part, bf16),
+            dma((2, 3, 3)), dma((2, 3, 3)), dma((3,)),
             dma((2, 2)), dma((2, 2)),
             pltpu.SemaphoreType.REGULAR,
             dma((3,)), dma((3,)), dma((4, 3)), dma((4, 3)),
-            dma((4, 3)), dma((4, 3)), dma((2, 3)), dma((2, 3)), dma((2,)), dma((2,)), dma, dma,
+            dma((4, 2, 3)), dma((4, 2, 3)), dma((2,)), dma((2,)), dma, dma,
             dma((2,)), dma((2,)),
             dma((3,)), dma((3,)),
         ],

time: 102 us -> 100 us (0.980)
  Pallas kernels: 96.7 us -> 95.6 us
    pallas_call x1, Pallas kernels: 96.7 us -> 95.6 us  [body(): pl.pallas_call(kernel, out_shape=(jax.ShapeDtypeStruct((128, 4096), bf16)...]
where the time goes in v6:
time: 100 us; the launch traced here: 99.9 us
  Pallas kernels  95.6 us (96%)
  local copies, waits for them, and re-layouts  3.68 us (4%)
    pallas_call x1, Pallas kernels, body(): pl.pallas_call(kernel, out_shape=(jax.ShapeDtypeStruct((128, 4096), bf16)...  95.6 us
    unnamed x7, local copies, waits for them, and re-layouts  3.68 us

profile of v6, /device:TPU:1, one launch (start us, length us, event | category | flops | bytes accessed | tf_op | source)
XLA Modules:
  0.0 99.9 jit_solution(11544809975490783425)
XLA Ops:
  0.6 95.6 %shard_map.67 = (bf16[128,4096]{1,0:T(8,128)(2,1)}, bf16[128,128]{1,0:T(8,128)(2,1)}, bf16[128,128]{1,0:T(8,128)(2,1)}) custom-call(bf16[128,4096]{1,0:T(8,128)(2,1)} %bitcast.4, bf16[128,128]{1,0:T(8,128)(2,1)} %k_in.1, bf16[128,128]{1,0:T(8,128)(2,1)} %v_in.1, bf16[128,4096]{1,0:T(8,128)(2,1)} %bitcast.5), custom_call_target="tpu_custom_call" | custom-call | flops 16000000000 | bytes 4194304 | tf_op jit(solution)/shard_map/pallas_call | solution.py:450
  96.2 0.0 copy-start.1
  96.2 2.3 %copy.10 = bf16[1,128,4096]{2,1,0:T(8,128)(2,1)} copy(bf16[1,128,4096]{2,1,0:T(8,128)(2,1)} %bitcast.3) | data formatting | bytes 2097152
  98.5 0.0 copy-done.1
  98.5 0.0 copy-start
  98.5 0.6 copy.11
  99.1 0.2 copy-done
  99.3 0.6 copy.12
Async XLA Ops:
  96.2 2.3 %copy-start.1 = (bf16[128,128]{1,0:T(8,128)(2,1)S(1)}, bf16[128,128]{1,0:T(8,128)(2,1)}, u32[]{:S(2)}) copy-start(bf16[128,128]{1,0:T(8,128)(2,1)} %get-tuple-element.13) | copy-start | bytes 98308
  98.5 0.8 copy-start

commit v7 on v6

--- a/solution.py
+++ b/solution.py
@@ -390,7 +390,7 @@
             when(o == 2 * h + 1, lambda: along_z(g, h, (0,)))
 
     def second_rows(o, carry):
-        when(o == 8, lambda: over_free(0))
+        when(o == 10, lambda: over_free(0))
         for blk in range(2):
             chunk(grads, blk, chunk_at(3 - o // 4, o % 4), [2 * blk, 2 * blk + 1])
         send_parts(3 - o // 4, o % 4)
@@ -399,9 +399,9 @@
     lax.fori_loop(0, 12, second_rows, 0)
 
     def third_rows(o, carry):
-        when(o == 0, lambda: over_free(1))
+        when(o == 4, lambda: over_free(1))
         when(
-            o == 4, over_cross,
+            o == 4,
             lambda: finish(3 - core), lambda: back[2].start(),
             lambda: finish(1 - core), lambda: back[0].start(),
         )
@@ -412,6 +412,7 @@
         return carry
 
     lax.fori_loop(0, 8, third_rows, 0)
+    over_cross()
     finish(2 + core)
     back[1].start()
     finish(core)

time: 100 us -> 97.1 us (0.971); the launches traced: 99.9 us -> 95.5 us
  Pallas kernels: 95.6 us -> 91.2 us
    pallas_call x1, Pallas kernels: 95.6 us -> 91.2 us  [body(): pl.pallas_call(kernel, out_shape=(jax.ShapeDtypeStruct((128, 4096), bf16)...]
where the time goes in v7:
time: 97.1 us; the launch traced here: 95.5 us
  Pallas kernels  91.2 us (94%)
  local copies, waits for them, and re-layouts  3.68 us (4%)
    pallas_call x1, Pallas kernels, body(): pl.pallas_call(kernel, out_shape=(jax.ShapeDtypeStruct((128, 4096), bf16)...  91.2 us
    unnamed x7, local copies, waits for them, and re-layouts  3.68 us

profile of v7, /device:TPU:1, one launch (start us, length us, event | category | flops | bytes accessed | tf_op | source)
XLA Modules:
  0.0 95.5 jit_solution(17662360975453702610)
XLA Ops:
  0.6 91.2 %shard_map.67 = (bf16[128,4096]{1,0:T(8,128)(2,1)}, bf16[128,128]{1,0:T(8,128)(2,1)}, bf16[128,128]{1,0:T(8,128)(2,1)}) custom-call(bf16[128,4096]{1,0:T(8,128)(2,1)} %bitcast.4, bf16[128,128]{1,0:T(8,128)(2,1)} %k_in.1, bf16[128,128]{1,0:T(8,128)(2,1)} %v_in.1, bf16[128,4096]{1,0:T(8,128)(2,1)} %bitcast.5), custom_call_target="tpu_custom_call" | custom-call | flops 16000000000 | bytes 4194304 | tf_op jit(solution)/shard_map/pallas_call | solution.py:451
  91.8 0.0 copy-start.1
  91.8 2.3 %copy.10 = bf16[1,128,4096]{2,1,0:T(8,128)(2,1)} copy(bf16[1,128,4096]{2,1,0:T(8,128)(2,1)} %bitcast.3) | data formatting | bytes 2097152
  94.1 0.0 copy-done.1
  94.1 0.0 copy-start
  94.1 0.6 copy.11
  94.7 0.2 copy-done
  94.9 0.6 copy.12
Async XLA Ops:
  91.8 2.3 %copy-start.1 = (bf16[128,128]{1,0:T(8,128)(2,1)S(1)}, bf16[128,128]{1,0:T(8,128)(2,1)}, u32[]{:S(2)}) copy-start(bf16[128,128]{1,0:T(8,128)(2,1)} %get-tuple-element.13) | copy-start | bytes 98308
  94.1 0.8 copy-start

commit v8 on v7

--- a/solution.py
+++ b/solution.py
@@ -58,7 +58,7 @@
     z_up, z_dn = dev(x_hi, core, x_lo, y, (z + 1) % 4), dev(x_hi, core, x_lo, y, (z + 3) % 4)
     y_step = 1 - 2 * (y % 2)
     y_all = (dev(x_hi, core, x_lo, 3 - y, z), dev(x_hi, core, x_lo, y + y_step, z))
-    gate = [mates[0], dev(x_hi, core, 1 - x_lo, y, z), dev(x_hi, 1 - core, 1 - x_lo, y, z)]
+    gate = [dev(x_hi, core, 1 - x_lo, y, z), dev(x_hi, 1 - core, 1 - x_lo, y, z)]
     z_all = (z_up, z_dn, dev(x_hi, core, x_lo, y, (z + 2) % 4))
 
     def x_to(t):
@@ -68,7 +68,7 @@
         return dev(x_lo, core, s, y, z)
 
     barrier = pltpu.get_barrier_semaphore()
-    for peer in mates + list(y_all + z_all) + gate[1:]:
+    for peer in mates + list(y_all + z_all) + gate:
         pl.semaphore_signal(barrier, inc=1, device_id=peer, device_id_type=pl.DeviceIdType.MESH)
     for t in range(2):
         @pl.when(jnp.logical_not(jnp.logical_and(t == x_hi, x_lo == x_hi)))
@@ -190,7 +190,7 @@
     y_copies[1].wait_recv()
     for copy in z_sent[2]:
         copy.start()
-    pl.semaphore_wait(clear_sem, 3)
+    pl.semaphore_wait(clear_sem, 2)
     for piece in (1, 2):
         for n in (1, 2):
             for copy in ex[n][piece]:
@@ -400,6 +400,7 @@
 
     def third_rows(o, carry):
         when(o == 4, lambda: over_free(1))
+        when(o == 7, over_cross)
         when(
             o == 4,
             lambda: finish(3 - core), lambda: back[2].start(),
@@ -412,7 +413,6 @@
         return carry
 
     lax.fori_loop(0, 8, third_rows, 0)
-    over_cross()
     finish(2 + core)
     back[1].start()
     finish(core)

time: 97.1 us -> 97.1 us (level)
  no operation moved by 1% of the time
where the time goes in v8:
time: 97.1 us; the launch traced here: 95.5 us
  Pallas kernels  91.2 us (94%)
  local copies, waits for them, and re-layouts  3.68 us (4%)
    pallas_call x1, Pallas kernels, body(): pl.pallas_call(kernel, out_shape=(jax.ShapeDtypeStruct((128, 4096), bf16)...  91.2 us
    unnamed x7, local copies, waits for them, and re-layouts  3.68 us

profile of v8, /device:TPU:1, one launch (start us, length us, event | category | flops | bytes accessed | tf_op | source)
XLA Modules:
  0.0 95.5 jit_solution(12934754299079221211)
XLA Ops:
  0.6 91.2 %shard_map.67 = (bf16[128,4096]{1,0:T(8,128)(2,1)}, bf16[128,128]{1,0:T(8,128)(2,1)}, bf16[128,128]{1,0:T(8,128)(2,1)}) custom-call(bf16[128,4096]{1,0:T(8,128)(2,1)} %bitcast.4, bf16[128,128]{1,0:T(8,128)(2,1)} %k_in.1, bf16[128,128]{1,0:T(8,128)(2,1)} %v_in.1, bf16[128,4096]{1,0:T(8,128)(2,1)} %bitcast.5), custom_call_target="tpu_custom_call" | custom-call | flops 16000000000 | bytes 4194304 | tf_op jit(solution)/shard_map/pallas_call | solution.py:451
  91.8 0.0 copy-start.1
  91.8 2.3 %copy.10 = bf16[1,128,4096]{2,1,0:T(8,128)(2,1)} copy(bf16[1,128,4096]{2,1,0:T(8,128)(2,1)} %bitcast.3) | data formatting | bytes 2097152
  94.1 0.0 copy-done.1
  94.1 0.0 copy-start
  94.1 0.6 copy.11
  94.7 0.2 copy-done
  94.9 0.6 copy.12
Async XLA Ops:
  91.8 2.3 %copy-start.1 = (bf16[128,128]{1,0:T(8,128)(2,1)S(1)}, bf16[128,128]{1,0:T(8,128)(2,1)}, u32[]{:S(2)}) copy-start(bf16[128,128]{1,0:T(8,128)(2,1)} %get-tuple-element.13) | copy-start | bytes 98308
  94.1 0.8 copy-start

commit v9 on v7

--- a/solution.py
+++ b/solution.py
@@ -144,7 +144,7 @@
                 away.start()
 
     def exchange(n, piece):
-        start, width = ((0, 256), (256, 256), (512, 512))[piece]
+        start, width = ((0, 128), (128, 384), (512, 512))[piece]
         c_t, flip = ((1 - core, 0), (core, 1), (1 - core, 1))[n]
         x_t = (1 - x_lo) if flip else x_lo
         cols = lanes((2 * x_t + c_t) * 1024 + start, width)
@@ -390,7 +390,6 @@
             when(o == 2 * h + 1, lambda: along_z(g, h, (0,)))
 
     def second_rows(o, carry):
-        when(o == 10, lambda: over_free(0))
         for blk in range(2):
             chunk(grads, blk, chunk_at(3 - o // 4, o % 4), [2 * blk, 2 * blk + 1])
         send_parts(3 - o // 4, o % 4)
@@ -399,7 +398,8 @@
     lax.fori_loop(0, 12, second_rows, 0)
 
     def third_rows(o, carry):
-        when(o == 4, lambda: over_free(1))
+        when(o == 1, lambda: over_free(0))
+        when(o == 6, lambda: over_free(1))
         when(
             o == 4,
             lambda: finish(3 - core), lambda: back[2].start(),

time: 97.1 us -> 97.2 us (level)
  no operation moved by 1% of the time
where the time goes in v9:
time: 97.2 us; the launch traced here: 95.3 us
  Pallas kernels  90.9 us (94%)
  local copies, waits for them, and re-layouts  3.68 us (4%)
    pallas_call x1, Pallas kernels, body(): pl.pallas_call(kernel, out_shape=(jax.ShapeDtypeStruct((128, 4096), bf16)...  90.9 us
    unnamed x7, local copies, waits for them, and re-layouts  3.68 us

profile of v9, /device:TPU:1, one launch (start us, length us, event | category | flops | bytes accessed | tf_op | source)
XLA Modules:
  0.0 95.3 jit_solution(8170591593362863519)
XLA Ops:
  0.6 90.9 %shard_map.67 = (bf16[128,4096]{1,0:T(8,128)(2,1)}, bf16[128,128]{1,0:T(8,128)(2,1)}, bf16[128,128]{1,0:T(8,128)(2,1)}) custom-call(bf16[128,4096]{1,0:T(8,128)(2,1)} %bitcast.4, bf16[128,128]{1,0:T(8,128)(2,1)} %k_in.1, bf16[128,128]{1,0:T(8,128)(2,1)} %v_in.1, bf16[128,4096]{1,0:T(8,128)(2,1)} %bitcast.5), custom_call_target="tpu_custom_call" | custom-call | flops 16000000000 | bytes 4194304 | tf_op jit(solution)/shard_map/pallas_call | solution.py:451
  91.6 0.0 copy-start.1
  91.6 2.3 %copy.10 = bf16[1,128,4096]{2,1,0:T(8,128)(2,1)} copy(bf16[1,128,4096]{2,1,0:T(8,128)(2,1)} %bitcast.3) | data formatting | bytes 2097152
  93.9 0.0 copy-done.1
  93.9 0.0 copy-start
  93.9 0.6 copy.11
  94.5 0.2 copy-done
  94.7 0.6 copy.12
Async XLA Ops:
  91.6 2.3 %copy-start.1 = (bf16[128,128]{1,0:T(8,128)(2,1)S(1)}, bf16[128,128]{1,0:T(8,128)(2,1)}, u32[]{:S(2)}) copy-start(bf16[128,128]{1,0:T(8,128)(2,1)} %get-tuple-element.13) | copy-start | bytes 98308
  93.9 0.8 copy-start
